TPU v7x, 128 devices: a whole 4x4x4 slice. The times are simulated.
128 devices in a mesh: gx: 4 (over y), gy: 32 (over x, z, core).
Axes of the slice: x: 4, y: 4, z: 4, core: 2. Of those that a mesh axis runs over, the one named last changes fastest.
Arguments:
- blocks: float32 [4096, 8, 128, 128], P(('gx', 'gy')), may hold values from -0.1875 to 0.1875
- columns: int32 [4096, 8], P(('gx', 'gy')), may hold values from 0 to 4095, as said below
- counts: int32 [4096], P(('gx', 'gy')), may hold values from 2 to 8, as said below
- start_vectors: float32 [524288, 256], P(('gx', 'gy')), may hold values from -6 to 6
Outputs:
- basis: float32 [524288, 256], P(('gx', 'gy'))
- factor: float32 [256, 256], replicated
Inputs may be any that keep to these rules, and one draw needn't show every extreme that they name: `columns`: slots below a row's count name distinct block rows within 4 of the row, slot 0 the row itself; slots at or past the count hold the row's own index. `counts`: some block row has exactly 8 live slots.
All inputs are finite; a program needn't handle non-finite values.
Results may differ from a plain program's by a relative error of at most 0.0003.
Values sent between devices are 32-bit elements; how exact they have to be, the bound alone decides.
No kernel may reach another device: no remote copies, remote signals or barrier semaphores. Data moves between devices by JAX's collectives and lax.ppermute only.
A program may use at most 192 MiB of HBM per device.

v0:
```python
import jax
import jax.numpy as jnp
from jax import lax
from jax.sharding import PartitionSpec as P

REACH = 4
DEGREE = 3


def padded(cells, sides, width):
    for axis, dim in sides:
        count = lax.axis_size(axis)
        ends = count - 1
        head = lax.slice_in_dim(cells, 0, width, axis=dim)
        tail = lax.slice_in_dim(cells, cells.shape[dim] - width, cells.shape[dim], axis=dim)
        cells = jnp.concatenate(
            [
                lax.ppermute(tail, axis, [(i, (i + 1) % count) for i in range(ends)]),
                cells,
                lax.ppermute(head, axis, [((i + 1) % count, i) for i in range(ends)]),
            ],
            axis=dim,
        )
    return cells


def shifted(value, axis, steps):
    count = lax.axis_size(axis)
    first, last = (max(0, -steps), min(count, count - steps))
    return lax.ppermute(value, axis, [(source, source + steps) for source in range(first, last)])


def vector_rim(vectors):
    rows_here = vectors.shape[0]
    size_b = vectors.shape[1]
    flat = vectors.reshape(rows_here * size_b, -1)
    extended = padded(flat, ((("gx", "gy"), 0),), REACH * size_b)
    return extended.reshape(-1, size_b, vectors.shape[2])


def apply_returned(vectors, blocks, columns, counts, first_row):
    rows_here = blocks.shape[0]
    size_b = blocks.shape[2]
    extended = vector_rim(vectors)
    source_index = columns - first_row + REACH
    busiest = jnp.max(counts)
    forward_init = jnp.zeros_like(vectors)
    returned_init = jnp.zeros((rows_here + 2 * REACH, size_b, vectors.shape[2]), jnp.float32)

    def one_slot(slot, state_pair):
        forward, returned = state_pair
        live_mask = (slot < counts).astype(jnp.float32)[:, None, None]
        block = blocks[:, slot]
        fetched = extended[source_index[:, slot]]
        forward = forward + live_mask * jnp.einsum(
            "nab,nbk->nak", block, fetched, precision=lax.Precision.HIGHEST
        )
        moved = live_mask * jnp.einsum(
            "nba,nbk->nak", block, vectors, precision=lax.Precision.HIGHEST
        )
        returned = returned.at[source_index[:, slot]].add(moved)
        return (forward, returned)

    forward, returned = lax.fori_loop(0, busiest, one_slot, (forward_init, returned_init))
    from_next = shifted(returned[:REACH], ("gx", "gy"), -1)
    from_prior = shifted(returned[rows_here + REACH :], ("gx", "gy"), 1)
    own_part = returned[REACH : rows_here + REACH]
    own_part = own_part.at[:REACH].add(from_prior)
    own_part = own_part.at[rows_here - REACH :].add(from_next)
    return 0.5 * (forward + own_part)


def body(blocks, columns, counts, start_vectors):
    rows_here = blocks.shape[0]
    size_b = blocks.shape[2]
    width_k = start_vectors.shape[1]
    first_row = lax.axis_index(("gx", "gy")) * rows_here

    def operate(vectors):
        return apply_returned(vectors, blocks, columns, counts, first_row)

    prior = start_vectors.reshape(rows_here, size_b, width_k)
    current = operate(prior)
    for level in range(DEGREE - 1):
        following = 2.0 * operate(current) - prior
        prior, current = (current, following)
    filtered = current.reshape(rows_here * size_b, width_k)
    gram_total = lax.psum(
        jnp.dot(filtered.T, filtered, precision=lax.Precision.HIGHEST), ("gx", "gy")
    )
    lower = jnp.linalg.cholesky(gram_total)
    identity = jnp.eye(width_k, dtype=jnp.float32)
    inverse_upper = jax.scipy.linalg.solve_triangular(lower, identity, lower=True).T
    orthonormal = jnp.dot(filtered, inverse_upper, precision=lax.Precision.HIGHEST)
    total_rows = rows_here * size_b * lax.axis_size(("gx", "gy"))
    scale_root = jnp.sqrt(jnp.float32(total_rows))
    return (orthonormal * scale_root, lower.T / scale_root)


def solution(mesh):
    placed = (
        P(("gx", "gy"), None, None, None),
        P(("gx", "gy"), None),
        P(("gx", "gy")),
        P(("gx", "gy"), None),
    )
    return jax.shard_map(
        body, mesh=mesh, in_specs=placed, out_specs=(P(("gx", "gy"), None), P()), check_vma=False
    )
```

profile of v0, /device:TPU:1, one launch (start us, length us, event | category | flops | bytes accessed | tf_op | source)
XLA Modules:
  0.0 1219.9 jit_solution(7489490828775388821)
XLA Ops:
  15.4 11.7 copy.11
  38.0 279.2 %while.43 = (s32[]{:T(128)}, f32[32,128,256]{2,1,0:T(8,128)}, f32[40,128,256]{2,1,0:T(8,128)}, s32[]{:T(128)}, s32[32]{0:T(128)S(1)}, /*index=5*/f32[32,8,128,12...) while((s32[]{:T(128)}, f32[32,128,256]{2,1,0:T(8,128)}, ...), condition=%wide.region_3.0_spmd, body=%wide.region_1.0_spmd.sunk | while | flops 3225420800 | bytes 46142760 | solution.py:64
  47.6 10.2 scatter_fusion
  63.1 10.1 multiply_add_fusion.6
  97.9 10.1 multiply_add_fusion.6
  167.2 10.1 multiply_add_fusion.6
  202.1 10.1 multiply_add_fusion.6
  359.8 277.5 %while.44 = (s32[]{:T(128)}, f32[32,128,256]{2,1,0:T(8,128)}, f32[40,128,256]{2,1,0:T(8,128)}, s32[]{:T(128)}, s32[32]{0:T(128)S(1)}, /*index=5*/f32[32,8,128,12...) while((s32[]{:T(128)}, f32[32,128,256]{2,1,0:T(8,128)}, ...), condition=%wide.region_6.0_spmd, body=%wide.region_4.6_spmd.sunk | while | flops 3225420800 | bytes 46142760 | solution.py:64
  369.2 10.2 scatter_fusion.1
  453.7 10.1 multiply_add_fusion.7
  488.1 10.1 multiply_add_fusion.7
  522.7 10.1 multiply_add_fusion.7
  677.9 277.7 %while.45 = (s32[]{:T(128)}, f32[32,128,256]{2,1,0:T(8,128)}, f32[40,128,256]{2,1,0:T(8,128)}, s32[]{:T(128)}, s32[32]{0:T(128)S(1)}, /*index=5*/f32[32,8,128,12...) while((s32[]{:T(128)}, f32[32,128,256]{2,1,0:T(8,128)}, ...), condition=%wide.region_9.0_spmd, body=%wide.region_7.0_spmd.sunk | while | flops 3225420800 | bytes 46142760 | solution.py:64
  687.3 10.2 scatter_fusion.2
  702.8 10.1 multiply_add_fusion.8
  737.3 10.1 multiply_add_fusion.8
  771.8 10.1 multiply_add_fusion.8
  840.9 10.1 multiply_add_fusion.8
  875.6 10.1 multiply_add_fusion.8
  910.2 10.1 multiply_add_fusion.8
  980.8 160.5 %all-reduce.3.cloned.1.call-done = f32[256,256]{0,1:T(8,128)} async-done(((f32[256,256]{0,1:T(8,128)}), f32[256,256]{0,1:T(8,128)}) %all-reduce.3.cloned.1.call-update) | async-done | bytes 262160 | tf_op jit(solution)/shard_map/psum | solution.py:88
  1143.4 12.1 cholesky.50
  1165.8 11.7 cholesky.105
  1183.8 19.7 %custom-call.16 = f32[2,128,128]{1,2,0:T(8,128)S(1)} custom-call(f32[2,128,128]{2,1,0:T(8,128)S(1)} %get-tuple-element.234), custom_call_target="InvertDiagBlocksLowerTriangular" | custom-call | tf_op jit(solution)/shard_map/jit(_solve_triangular)/triangular_solve | solution.py:93
  (255 shorter events, 814.5 us)
Async XLA Ops:
  7.2 1134.1 %all-reduce.3.cloned.1.call-start = ((), (), s32[]{:S(2)}) async-start(), calls=%async_computation | async-start | bytes 524288 | tf_op jit(solution)/shard_map/psum | solution.py:88
  8.5 19.2 %collective-permute-start = (f32[512,256]{1,0:T(8,128)S(1)}, f32[512,256]{1,0:T(8,128)S(1)}, u32[]{:S(2)}, u32[]{:S(2)}) collective-permute-start(f32[512,256]{1,0:T(8,128)S(1)} %get-tuple-element.338), channel_id=1, source_target_pairs={{0,1},{1,2},{2,3},{3,4},{4,5},{5,6},{6,7},{7,8},{8,9},{9,10},{10,1... | collective-permute-start | bytes 1572872 | tf_op jit(solution)/shard_map/ppermute | solution.py:18
  13.4 14.3 %collective-permute-start.1 = (f32[512,256]{1,0:T(8,128)S(1)}, f32[512,256]{1,0:T(8,128)S(1)}, u32[]{:S(2)}, u32[]{:S(2)}) collective-permute-start(f32[512,256]{1,0:T(8,128)S(1)} %get-tuple-element.339), channel_id=1, source_target_pairs={{1,0},{2,1},{3,2},{4,3},{5,4},{6,5},{7,6},{8,7},{9,8},{10,9},{11,1... | collective-permute-start | bytes 1572872 | tf_op jit(solution)/shard_map/ppermute | solution.py:20
  15.4 11.7 copy-start.9
  15.4 12.3 %copy-start.8 = (s32[32,8]{0,1:T(8,128)S(1)}, s32[32,8]{0,1:T(8,128)}, u32[]{:S(2)}) copy-start(s32[32,8]{0,1:T(8,128)} %param.23) | copy-start | bytes 3076
  318.6 8.0 collective-permute-start.2
  320.5 10.9 copy-start.4
  320.6 10.8 collective-permute-start.3
  332.3 2.1 copy-start
  334.4 8.0 collective-permute-start.4
  336.4 13.1 %collective-permute-start.5 = (f32[512,256]{1,0:T(8,128)S(1)}, f32[512,256]{1,0:T(8,128)S(1)}, u32[]{:S(2)}, u32[]{:S(2)}) collective-permute-start(f32[512,256]{1,0:T(8,128)S(1)} %bitcast.113), channel_id=1, source_target_pairs={{1,0},{2,1},{3,2},{4,3},{5,4},{6,5},{7,6},{8,7},{9,8},{10,9},{11,1... | collective-permute-start | bytes 1572872 | tf_op jit(solution)/shard_map/ppermute | solution.py:20
  638.6 8.0 collective-permute-start.6
  640.5 10.9 copy-start.2
  640.5 10.9 copy-start.5
  640.5 10.8 collective-permute-start.7
  652.7 1.9 copy-start.3
  654.7 8.0 collective-permute-start.8
  656.6 10.9 collective-permute-start.9
  956.9 8.0 collective-permute-start.10
  958.8 10.9 copy-start.1
  958.8 10.9 copy-start.6
  958.8 10.8 collective-permute-start.11
  971.0 1.9 copy-start.7
Sparse Core Ops, SparseCore 0:
  980.8 160.4 all-reduce.2
where the time goes:
time: 1230 us; the launch traced here: 1220 us
  matrix products  471 us (38%)
  other arithmetic  315 us (26%)
  waiting for transfers between devices  192 us (16%)
  local copies, waits for them, and re-layouts  180 us (15%)
  starting transfers between devices  30.6 us (2%)
  loops' own time  16.1 us (1%)
  between operations  16 us (1%)
    dot_general x24, matrix products, one_slot(): jnp.einsum('nab,nbk->nak', block, fetched, precision=lax.Precision.HIGHEST)  242 us
    scatter-add x24, other arithmetic, one_slot(): returned = returned.at[source_index[:, slot]].add(moved)  237 us
    dot_general x24, matrix products, one_slot(): jnp.einsum('nba,nbk->nak', block, vectors, precision=lax.Precision.HIGHEST)  212 us
    psum x1, waiting for transfers between devices, body(): lax.psum(jnp.dot(filtered.T, filtered, precision=lax.Precision.HIGHEST),...  161 us
    gather x24, local copies, waits for them, and re-layouts, one_slot(): fetched = extended[source_index[:, slot]]  127 us
    another operation x6, other arithmetic, body(): lower = jnp.linalg.cholesky(gram_total)  34.3 us
  transfers between devices with their start and end apart: 13, of which 11 were waited for; matrix products, arithmetic and copies ran while one was open for 2% of the time, Pallas kernels for 0%

commit v1 on v0

v1 whole, which is shorter than its diff:
```python
import jax
import jax.numpy as jnp
from jax import lax
from jax.experimental import pallas as pl
from jax.experimental.pallas import tpu as pltpu
from jax.sharding import Mesh, PartitionSpec as P

B = 128
K = 256
ROWS = 32
SLOTS = 8
REACH = 4
PANELS = ROWS // 2
WIDE = 10 * B
EDGE = REACH * B
LOCAL = ROWS * B
EXT = LOCAL + 2 * EDGE
DEAD = ROWS * SLOTS
TABLE = (ROWS + 10) * 16
RING = 16
VRING = 6
KEPT = 4
PAIRS_PREV = [(r, o) for r in range(4) for o in range(-4, 0) if r + o < 0]
PAIRS_NEXT = [(r, o) for r in range(28, 32) for o in range(1, 5) if r + o > 31]
PACKED = 10 * B + 2 * EDGE

F32 = jnp.float32
BF16 = jnp.bfloat16
VM = pl.BlockSpec(memory_space=pltpu.VMEM)
SM = pl.BlockSpec(memory_space=pltpu.SMEM)
HB = pl.BlockSpec(memory_space=pltpu.HBM)
ALL = ("y", "x", "z", "c")


def params(mib):
    return pltpu.CompilerParams(vmem_limit_bytes=mib * 2**20)


def cost(flops, moved):
    return pl.CostEstimate(flops=int(flops), bytes_accessed=int(moved), transcendentals=0)


def dot(a, b):
    return jnp.dot(a, b, preferred_element_type=F32)


def split(x):
    high = x.astype(BF16)
    return high, (x - high.astype(F32)).astype(BF16)


def rows(start, size):
    return pl.ds(pl.multiple_of(start, size), size)


def place(r, o):
    return (r + 5) * 16 + o + 5


def fill_table(table, columns, counts, first, r):
    for s in range(SLOTS):
        offset = columns[s, r] - first - r
        table[jnp.where(s < counts[r], place(r, offset), TABLE)] = r * SLOTS + s


def clear_table(table, start, stop):
    for k in range(start, stop):
        table[k] = DEAD


def even_core(columns):
    return (columns[0, 0] // ROWS) % 2 == 0


def pack_kernel(columns, counts, blocks, vectors, swap_far, swap_near, table, zero, sems):
    first = columns[0, 0]
    zero[...] = jnp.zeros_like(zero)
    for r in (0, 1, 2, 3, 28, 29, 30, 31):
        clear_table(table, place(r, -4), place(r, 5))
        fill_table(table, columns, counts, first, r)

    def fill(to_prev, to_next):
        moves = []
        for side, (out, pairs) in enumerate(((to_prev, PAIRS_PREV), (to_next, PAIRS_NEXT))):
            start = 0 if side == 0 else LOCAL - EDGE
            for half in range(2):
                move = pltpu.make_async_copy(
                    vectors.at[pl.ds(start, EDGE), pl.ds(half * B, B)],
                    out.at[pl.ds(10 * B + half * EDGE, EDGE), :],
                    sems.at[side * 12 + 10 + half],
                )
                move.start()
                moves.append(move)
            for k, (r, o) in enumerate(pairs):
                slot = table[place(r, o)]
                target = out.at[pl.ds(k * B, B), :]
                sem = sems.at[side * 12 + k]

                @pl.when(slot < DEAD)
                def _():
                    pltpu.make_async_copy(blocks.at[slot], target, sem).start()

                @pl.when(slot >= DEAD)
                def _():
                    pltpu.make_async_copy(zero, target, sem).start()

                moves.append(pltpu.make_async_copy(zero, target, sem))
        for move in moves:
            move.wait()

    even = even_core(columns)

    @pl.when(even)
    def _():
        fill(swap_far, swap_near)

    @pl.when(jnp.logical_not(even))
    def _():
        fill(swap_near, swap_far)


def apply_panel(p, hh, hl, vh, vl):
    window = pl.ds(pl.multiple_of(p * 2 * B, 2 * B), WIDE)
    return dot(hh, vh[window, :]) + dot(hl, vh[window, :]) + dot(hh, vl[window, :])


def store_rows(p, value, uh, ul, part):
    at = rows(EDGE + p * 2 * B, 2 * B)
    uh[at, :], ul[at, :] = split(value)
    spare = jnp.where(p < 2, p, jnp.where(p >= PANELS - 2, p - PANELS + 4, 4))
    part[rows(spare * 2 * B, 2 * B), :] = value


def clear_pads(*refs):
    for ref in refs:
        ref[:EDGE, :] = jnp.zeros((EDGE, K), BF16)
        ref[EXT - EDGE :, :] = jnp.zeros((EDGE, K), BF16)


def first_kernel(
    columns, counts, blocks, vectors, hh, hl, vh, vl, uh, ul, part, table, sbuf, vbuf, ah, al, bh, bl, ssem, vsem
):
    def block_copy(r):
        return pltpu.make_async_copy(
            blocks.at[pl.ds(r * SLOTS, SLOTS)],
            sbuf.at[rows((r % RING) * SLOTS, SLOTS)],
            ssem.at[r % RING],
        )

    def vector_copy(q):
        return pltpu.make_async_copy(
            vectors.at[rows(q * 2 * B, 2 * B), :], vbuf.at[q % VRING], vsem.at[q % VRING]
        )

    def take_vectors(q):
        vector_copy(q).wait()
        at = rows(EDGE + q * 2 * B, 2 * B)
        vh[at, :], vl[at, :] = split(vbuf[q % VRING])

    for q in range(VRING):
        block_copy(2 * q).start()
        block_copy(2 * q + 1).start()
        vector_copy(q).start()
    for r in range(2 * VRING, RING):
        block_copy(r).start()
    sbuf[RING * SLOTS] = jnp.zeros((B, B), F32)
    clear_pads(vh, vl, uh, ul)
    first = columns[0, 0]

    def clear(r, _):
        for k in range(16):
            table[r * 16 + k] = DEAD
        return 0

    def fill(r, _):
        fill_table(table, columns, counts, first, r)
        return 0

    lax.fori_loop(0, ROWS + 10, clear, 0)
    lax.fori_loop(0, ROWS, fill, 0)

    def fetch(slot, inside=True):
        return sbuf[jnp.where(inside & (slot < DEAD), slot % (RING * SLOTS), RING * SLOTS)]

    def build(p, high, low):
        for h in range(2):
            i = 2 * p + h
            at = slice(h * B, h * B + B)
            for c in range(10):
                o = c - 4 - h
                cols = slice(c * B, c * B + B)
                if abs(o) > REACH:
                    parts = (jnp.zeros((B, B), BF16),) * 2
                else:
                    near = fetch(table[place(i, o)], (i + o >= 0) & (i + o < ROWS))
                    far = fetch(table[place(i + o, -o)])
                    parts = split(near + far.T)
                high[at, cols], low[at, cols] = parts
                hh[p, at, cols], hl[p, at, cols] = parts

    def ready(p):
        @pl.when(p < PANELS - 2)
        def _():
            block_copy(2 * p + 4).wait()
            block_copy(2 * p + 5).wait()
            take_vectors(p + 2)

            @pl.when(p + 2 + VRING < PANELS)
            def _():
                vector_copy(p + 2 + VRING).start()

    def refill(p):
        @pl.when((p >= 3) & (p < PANELS - 5))
        def _():
            block_copy(2 * p + 10).start()
            block_copy(2 * p + 11).start()

    for r in range(REACH):
        block_copy(r).wait()
    for q in range(2):
        take_vectors(q)
        vector_copy(q + VRING).start()
    ready(0)
    build(0, ah, al)

    def step(t, _):
        p = 2 * t
        refill(p)
        refill(p + 1)
        ready(p + 1)
        ready(p + 2)
        first_half = 0.5 * apply_panel(p, ah[...], al[...], vh, vl)
        build(p + 1, bh, bl)
        store_rows(p, first_half, uh, ul, part)
        second_half = 0.5 * apply_panel(p + 1, bh[...], bl[...], vh, vl)
        build(jnp.minimum(p + 2, PANELS - 1), ah, al)
        store_rows(p + 1, second_half, uh, ul, part)
        return 0

    lax.fori_loop(0, PANELS // 2, step, 0)


def inner_kernel(hh, hl, vh, vl, ph, pr, uh, ul, part):
    clear_pads(uh, ul)

    def step(p, _):
        at = rows(EDGE + p * 2 * B, 2 * B)
        prior = ph[at, :].astype(F32) + pr[at, :].astype(F32)
        store_rows(p, apply_panel(p, hh[p], hl[p], vh, vl) - prior, uh, ul, part)
        return 0

    lax.fori_loop(0, PANELS, step, 0, unroll=2)


def cross(xh, xl, side, halo_high, halo_low):
    return dot(xh[side], halo_high) + dot(xl[side], halo_high) + dot(xh[side], halo_low)


def write_edge(side, value, uh, ul):
    start = EDGE if side == 0 else LOCAL
    uh[start : start + EDGE, :], ul[start : start + EDGE, :] = split(value)


def first_edge_kernel(
    columns, sent_far, sent_near, got_far, got_near, part, uh_in, ul_in, *rest
):
    uh, ul, xh, xl, far, near, own, got, sems = rest[KEPT:]
    del uh_in, ul_in
    even = even_core(columns)

    def fetch(refs):
        moves = [
            pltpu.make_async_copy(ref, place_, sems.at[k])
            for k, (ref, place_) in enumerate(zip(refs, (own.at[0], own.at[1], got.at[0], got.at[1])))
        ]
        for move in moves:
            move.start()
        for move in moves:
            move.wait()

    @pl.when(even)
    def _():
        fetch((sent_far, sent_near, got_far, got_near))

    @pl.when(jnp.logical_not(even))
    def _():
        fetch((sent_near, sent_far, got_near, got_far))

    zero = jnp.zeros((B, B), BF16)
    for r in range(REACH):
        for c in range(REACH):
            at, cols = slice(r * B, r * B + B), slice(c * B, c * B + B)
            if c >= r:
                a = PAIRS_PREV.index((r, c - 4 - r)) * B
                b = PAIRS_NEXT.index((28 + c, 4 + r - c)) * B
                value = own[0, a : a + B, :] + got[0, b : b + B, :].T
                xh[0, at, cols], xl[0, at, cols] = split(value)
            else:
                xh[0, at, cols], xl[0, at, cols] = zero, zero
            if c <= r:
                a = PAIRS_NEXT.index((28 + r, 4 + c - r)) * B
                b = PAIRS_PREV.index((c, r - c - 4)) * B
                value = own[1, a : a + B, :] + got[1, b : b + B, :].T
                xh[1, at, cols], xl[1, at, cols] = split(value)
            else:
                xh[1, at, cols], xl[1, at, cols] = zero, zero
    values = []
    for side in range(2):
        halves = [
            split(got[side, 10 * B + half * EDGE : 10 * B + (half + 1) * EDGE, :]) for half in range(2)
        ]
        high = jnp.concatenate([halves[0][0], halves[1][0]], axis=1)
        low = jnp.concatenate([halves[0][1], halves[1][1]], axis=1)
        value = part[side * EDGE : (side + 1) * EDGE, :] + 0.5 * cross(xh, xl, side, high, low)
        write_edge(side, value, uh, ul)
        values.append(value)
    send_edges(even, values, far, near)


def send_edges(even, values, far, near):
    far[...] = jnp.where(even, values[0], values[1])
    near[...] = jnp.where(even, values[1], values[0])


def finish_edges(columns, xh, xl, got_far, got_near, part, uh, ul):
    even = even_core(columns)
    a, b = got_far[...], got_near[...]
    values = []
    for side, halo in enumerate((jnp.where(even, a, b), jnp.where(even, b, a))):
        value = part[side * EDGE : (side + 1) * EDGE, :] + cross(xh, xl, side, *split(halo))
        write_edge(side, value, uh, ul)
        values.append(value)
    return even, values


def edge_kernel(columns, xh, xl, got_far, got_near, part, uh_in, ul_in, *rest):
    uh, ul, far, near = rest[KEPT:]
    del uh_in, ul_in
    even, values = finish_edges(columns, xh, xl, got_far, got_near, part, uh, ul)
    send_edges(even, values, far, near)


def last_edge_kernel(columns, xh, xl, got_far, got_near, part, uh_in, ul_in, uh, ul, mine, theirs):
    del uh_in, ul_in
    even, _ = finish_edges(columns, xh, xl, got_far, got_near, part, uh, ul)
    over = (((0,), (0,)), ((), ()))

    def step(q, totals):
        at = rows(EDGE + q * 512, 512)
        high, low = uh[at, :], ul[at, :]
        return (
            totals[0] + lax.dot_general(high, high, over, preferred_element_type=F32),
            totals[1] + lax.dot_general(high, low, over, preferred_element_type=F32),
        )

    zero = jnp.zeros((K, K), F32)
    main, mixed = lax.fori_loop(0, LOCAL // 512, step, (zero, zero))
    total = main + mixed + mixed.T
    r = lax.broadcasted_iota(jnp.int32, (B, B), 0)
    c = lax.broadcasted_iota(jnp.int32, (B, B), 1)
    corner, beside = total[B:, B:], total[:B, B:]
    square = jnp.where(c >= r, total[:B, :B], corner)
    diagonal = jnp.broadcast_to(jnp.sum(jnp.where(r == c, corner, 0.0), axis=0, keepdims=True), (8, B))
    none = jnp.zeros((8, B), F32)
    mine[:B, :] = jnp.where(even, square, beside)
    mine[B:, :] = jnp.where(even, diagonal, none)
    theirs[:B, :] = jnp.where(even, beside, square)
    theirs[B:, :] = jnp.where(even, none, diagonal)


def precise(a, b, over=(((1,), (0,)), ((), ()))):
    return lax.dot_general(
        a, b, over, precision=lax.Precision.HIGHEST, preferred_element_type=F32
    )


def basis_kernel(columns, mine, other, uh, ul, scale, basis, factor, work, upper, inverse, out, sems):
    r = lax.broadcasted_iota(jnp.int32, (B, B), 0)
    c = lax.broadcasted_iota(jnp.int32, (B, B), 1)
    even = even_core(columns)
    ad = jnp.where(even, mine[...], other[...])
    b = jnp.where(even, other[:B, :], mine[:B, :])
    square = ad[:B, :]
    high_part = jnp.where(c >= r, square, 0.0)
    low_part = jnp.where(c < r, square, 0.0)
    work[:B, :B] = high_part + jnp.where(c > r, square, 0.0).T
    work[:B, B:] = b
    work[B:, :B] = b.T
    work[B:, B:] = low_part + low_part.T + jnp.where(r == c, ad[B : B + 1, :], 0.0)

    r = lax.broadcasted_iota(jnp.int32, (K, K), 0)
    c = lax.broadcasted_iota(jnp.int32, (K, K), 1)
    gram = work[...]
    eye = jnp.where(r == c, 1.0, 0.0).astype(F32)
    on = jnp.where(r == c, gram, 0.0)
    row_d = jnp.sum(on, axis=0, keepdims=True)
    col_d = jnp.sum(on, axis=1, keepdims=True)
    row_s, col_s = lax.rsqrt(row_d), lax.rsqrt(col_d)
    scaled = gram * row_s * col_s
    work[...] = scaled
    gap = jnp.where(r == c, 0.0, scaled)

    def half_upper(e):
        return jnp.where(c > r, e, jnp.where(c == r, 0.5 * e, 0.0))

    left = (((0,), (0,)), ((), ()))

    def more(state):
        return (state[0] > 1e-8) & (state[0] < 4.0) & (state[1] < 12)

    def newton(state):
        _, count, y = state
        e = precise(y, precise(scaled, y), left) - eye
        return (jnp.sum(e * e), count + 1, y - precise(y, half_upper(e)))

    size, _, y = lax.while_loop(more, newton, (jnp.sum(gap * gap), 0, eye - half_upper(gap)))
    settled = (size <= 1e-8) & (jnp.min(jnp.where(r == c, y, 1.0)) > 0.0)

    @pl.when(settled)
    def _():
        inverse[...] = y
        full = precise(y, scaled, left)
        upper[...] = jnp.where(c >= r, full, 0.0)

    @pl.when(jnp.logical_not(settled))
    def _():
        lane = lax.broadcasted_iota(jnp.int32, (1, K), 1)
        down = lax.broadcasted_iota(jnp.int32, (K, 1), 0)

        def column(k, _):
            a = work[...]
            row = work[pl.ds(k, 1), :]
            root = lax.rsqrt(jnp.sum(jnp.where(lane == k, row, 0.0)))
            row = jnp.where(lane >= k, row * root, 0.0)
            col = jnp.sum(jnp.where(c == k, a, 0.0), axis=1, keepdims=True)
            col = jnp.where(down >= k, col * root, 0.0)
            upper[pl.ds(k, 1), :] = row
            work[...] = a - col * row
            return 0

        lax.fori_loop(0, K, column, 0)
        inverse[...] = jnp.zeros((K, K), F32)

        def back(t, _):
            k = K - 1 - t
            row = upper[pl.ds(k, 1), :]
            pivot = jnp.sum(jnp.where(lane == k, row, 0.0))
            rest = jnp.broadcast_to(jnp.where(lane > k, row, 0.0), (8, K))
            known = precise(rest, inverse[...])[:1, :]
            inverse[pl.ds(k, 1), :] = (jnp.where(lane == k, 1.0, 0.0) - known) / pivot
            return 0

        lax.fori_loop(0, K, back, 0)

    root = scale[0]
    factor[...] = upper[...] * (row_d * row_s) / root
    wh, wl = split(inverse[...] * (col_s * root))

    def out_copy(q):
        at = rows(q * 256, 256)
        return pltpu.make_async_copy(out.at[at, :], basis.at[at, :], sems.at[q])

    def step(q, _):
        at = rows(EDGE + q * 256, 256)
        out[rows(q * 256, 256), :] = dot(uh[at, :], wh) + dot(ul[at, :], wh) + dot(uh[at, :], wl)
        out_copy(q).start()
        return 0

    lax.fori_loop(0, LOCAL // 256, step, 0, unroll=2)
    for q in range(LOCAL // 256):
        out_copy(q).wait()


def swap_pairs(far, near):
    count = lax.axis_size(ALL)
    pairs = [(i, i + 1) for i in range(1, count - 1, 2)]
    got_far = lax.ppermute(far, ALL, pairs + [(j, i) for i, j in pairs])
    got_near = lax.ppermute(near, "c", [(0, 1), (1, 0)])
    return got_far, got_near


def group_sum(value, axis):
    count = lax.axis_size(axis)
    one, two, three = (
        lax.ppermute(value, axis, [(i, i ^ k) for i in range(count)]) for k in (1, 2, 3)
    )
    return (value + one) + (two + three)


def body(blocks, columns, counts, start_vectors):
    flat, start_vectors, counts, columns = (
        pltpu.with_memory_space_constraint(x, pltpu.HBM)
        for x in (blocks.reshape(DEAD, B, B), start_vectors, counts, columns.T)
    )
    packed = pltpu.HBM((PACKED, B), F32)
    sent = pl.pallas_call(
        pack_kernel,
        out_shape=(packed, packed),
        in_specs=(SM, SM, HB, HB),
        out_specs=(HB, HB),
        scratch_shapes=[
            pltpu.SMEM((TABLE + 1,), jnp.int32),
            pltpu.VMEM((B, B), F32),
            pltpu.SemaphoreType.DMA((24,)),
        ],
        compiler_params=params(2),
        cost_estimate=cost(0, 2 * 2 * PACKED * B * 4),
        name="pack_edges",
    )(columns, counts, flat, start_vectors)
    sent = [pltpu.with_memory_space_constraint(x, pltpu.HBM) for x in sent]
    got = swap_pairs(*sent)

    wide = pltpu.VMEM((PANELS, 2 * B, WIDE), BF16)
    slab = pltpu.VMEM((EXT, K), BF16)
    partial = pltpu.VMEM((10 * B, K), F32)
    crossing = pltpu.VMEM((2, EDGE, EDGE), BF16)
    edge = jax.ShapeDtypeStruct((EDGE, K), F32)
    flops = 3 * 2 * PANELS * 2 * B * WIDE * K
    hh, hl, vh, vl, uh, ul, part = pl.pallas_call(
        first_kernel,
        out_shape=(wide, wide, slab, slab, slab, slab, partial),
        in_specs=(SM, SM, HB, HB),
        out_specs=(VM,) * 7,
        scratch_shapes=[
            pltpu.SMEM((TABLE + 1,), jnp.int32),
            pltpu.VMEM((RING * SLOTS + 1, B, B), F32),
            pltpu.VMEM((VRING, 2 * B, K), F32),
        ]
        + [pltpu.VMEM((2 * B, WIDE), BF16)] * 4
        + [pltpu.SemaphoreType.DMA((RING,)), pltpu.SemaphoreType.DMA((VRING,))],
        compiler_params=params(14),
        cost_estimate=cost(flops * 2, 24 * 2**20),
        name="first_inner",
    )(columns, counts, flat, start_vectors)

    uh, ul, xh, xl, far, near = pl.pallas_call(
        first_edge_kernel,
        out_shape=(slab, slab, crossing, crossing, edge, edge),
        in_specs=(SM,) + (HB,) * 4 + (VM,) * (3 + KEPT),
        out_specs=(VM,) * 6,
        input_output_aliases={6: 0, 7: 1},
        scratch_shapes=[pltpu.VMEM((2, PACKED, B), F32)] * 2 + [pltpu.SemaphoreType.DMA((4,))],
        compiler_params=params(8),
        cost_estimate=cost(8e8, 6 * 2**20),
        name="first_edge",
    )(columns, *sent, *got, part, uh, ul, hh, hl, vh, vl)

    def inner(vectors, prior):
        return pl.pallas_call(
            inner_kernel,
            out_shape=(slab, slab, partial),
            in_specs=(VM,) * 6,
            out_specs=(VM,) * 3,
            compiler_params=params(6),
            cost_estimate=cost(flops, 2**20),
            name="inner",
        )(hh, hl, *vectors, *prior)

    got = swap_pairs(far, near)
    wh, wl, part = inner((uh, ul), (vh, vl))
    wh, wl, far, near = pl.pallas_call(
        edge_kernel,
        out_shape=(slab, slab, edge, edge),
        in_specs=(SM,) + (VM,) * (7 + KEPT),
        out_specs=(VM,) * 4,
        input_output_aliases={6: 0, 7: 1},
        compiler_params=params(8),
        cost_estimate=cost(8e8, 2 * 2**20),
        name="edge",
    )(columns, xh, xl, *got, part, wh, wl, hh, hl, uh, ul)

    got = swap_pairs(far, near)
    fh, fl, part = inner((wh, wl), (uh, ul))
    half = pltpu.VMEM((B + 8, B), F32)
    fh, fl, mine, theirs = pl.pallas_call(
        last_edge_kernel,
        out_shape=(slab, slab, half, half),
        in_specs=(SM,) + (VM,) * 7,
        out_specs=(VM,) * 4,
        input_output_aliases={6: 0, 7: 1},
        compiler_params=params(8),
        cost_estimate=cost(2e9, 2 * 2**20),
        name="last_edge_gram",
    )(columns, xh, xl, *got, part, fh, fl)

    swap = [(0, 1), (1, 0)]
    mine = mine + lax.ppermute(theirs, "c", swap)
    for axis in ("y", "x", "z"):
        mine = group_sum(mine, axis)
    other = lax.ppermute(mine, "c", swap)

    total_rows = LOCAL * lax.axis_size(ALL)
    scale = jnp.sqrt(jnp.float32(total_rows)).reshape(1)
    basis, factor = pl.pallas_call(
        basis_kernel,
        out_shape=(jax.ShapeDtypeStruct((LOCAL, K), F32), jax.ShapeDtypeStruct((K, K), F32)),
        in_specs=(SM, VM, VM, VM, VM, SM),
        out_specs=(HB, VM),
        scratch_shapes=[pltpu.VMEM((K, K), F32)] * 3
        + [pltpu.VMEM((LOCAL, K), F32), pltpu.SemaphoreType.DMA((LOCAL // 256,))],
        compiler_params=params(10),
        cost_estimate=cost(2e9, 4 * 2**20),
        name="basis",
    )(columns, mine, other, fh, fl, scale)
    return basis, factor


def solution(mesh):
    fine = Mesh(mesh.devices.reshape(4, 4, 4, 2), ALL)
    placed = (P(ALL, None, None, None), P(ALL, None), P(ALL), P(ALL, None))
    return jax.shard_map(
        body, mesh=fine, in_specs=placed, out_specs=(P(ALL, None), P()), check_vma=False
    )
```

time: 1230 us -> 271 us (0.22)
  matrix products: 471 us -> 0 us
  other arithmetic: 315 us -> 0.06 us
  Pallas kernels: 0 us -> 213 us
  waiting for transfers between devices: 192 us -> 10.9 us
  local copies, waits for them, and re-layouts: 180 us -> 1.36 us
  loops' own time: 16.1 us -> 0 us
  between operations: 16 us -> 0.98 us
    dot_general x50 -> x0, matrix products: 470 us -> none  [the longest x24 242 us: one_slot(): jnp.einsum('nab,nbk->nak', block, fetched, precision=lax.Precision.HIGHEST)]
    scatter-add x30 -> x0, other arithmetic: 241 us -> none  [the longest x24 237 us: one_slot(): returned = returned.at[source_index[:, slot]].add(moved)]
    pallas_call x0 -> x8, Pallas kernels: none -> 213 us  [the longest x1 118 us: body(): pl.pallas_call(basis_kernel, out_shape=(jax.ShapeDtypeStruct((LOCAL, K),...]
    psum x1 -> x0, waiting for transfers between devices: 161 us -> none  [body(): lax.psum(jnp.dot(filtered.T, filtered, precision=lax.Precision.HIGHEST),...]
    gather x24 -> x0, local copies, waits for them, and re-layouts: 127 us -> none  [one_slot(): fetched = extended[source_index[:, slot]]]
    another operation x8 -> x0, other arithmetic: 54 us -> none  [the longest x6 34.3 us: body(): lower = jnp.linalg.cholesky(gram_total)]
    another operation x15 -> x0, local copies, waits for them, and re-layouts: 20.5 us -> none
    ppermute x12 -> x17, waiting for transfers between devices: 31.3 us -> 10.9 us  [the longest x9 9.09 us: group_sum(): lax.ppermute(value, axis, [(i, i ^ k) for i in range(count)])]
  transfers between devices with their start and end apart: 13 -> 17, of which waited for: 11 -> 8; matrix products, arithmetic and copies ran while one was open for 2% -> 0% of each run, Pallas kernels for 0% -> 14%
where the time goes in v1:
time: 271 us; the launch traced here: 269 us
  Pallas kernels  213 us (79%)
  starting transfers between devices  42.6 us (16%)
  waiting for transfers between devices  10.9 us (4%)
    pallas_call x1, Pallas kernels, body(): pl.pallas_call(basis_kernel, out_shape=(jax.ShapeDtypeStruct((LOCAL, K),...  118 us
    pallas_call x1, Pallas kernels, body(): pl.pallas_call(pack_kernel, out_shape=(packed, packed), in_specs=(SM, SM,...  47.9 us
    ppermute x9, starting transfers between devices, group_sum(): lax.ppermute(value, axis, [(i, i ^ k) for i in range(count)])  24.3 us
    pallas_call x2, Pallas kernels, inner(): pl.pallas_call(inner_kernel, out_shape=(slab, slab, partial), in_specs=(V...  19.7 us
    pallas_call x1, Pallas kernels, body(): pl.pallas_call(first_kernel, out_shape=(wide, wide, slab, slab, slab, sla...  16.8 us
    ppermute x3, starting transfers between devices, swap_pairs(): got_far = lax.ppermute(far, ALL, pairs + [(j, i) for i, j in pairs])  12.6 us
    ppermute x9, waiting for transfers between devices, group_sum(): lax.ppermute(value, axis, [(i, i ^ k) for i in range(count)])  9.09 us
  transfers between devices with their start and end apart: 17, of which 8 were waited for; matrix products, arithmetic and copies ran while one was open for 0% of the time, Pallas kernels for 14%

profile of v1, /device:TPU:1, one launch (start us, length us, event | category | flops | bytes accessed | tf_op | source)
XLA Modules:
  0.0 269.2 jit_solution(13735449901708139374)
XLA Ops:
  0.6 47.9 %pack_edges.1 = (f32[2304,128]{1,0:T(8,128)}, f32[2304,128]{1,0:T(8,128)}) custom-call(s32[8,32]{1,0:T(8,128)} %bitcast.4, s32[32]{0:T(128)} %counts.3, f32[256,128,128]{2,1,0:T(8,128)} %bitcast.2, f32[4096,256]{1,0:T(8,128)} %vectors.3), custom_call_target="tpu_custom_call" | custom-call | bytes 4718592 | tf_op jit(solution)/shard_map/pack_edges/pallas_call | solution.py:496
  48.5 1.9 collective-permute-start
  50.5 16.8 %first_inner.1 = (bf16[16,256,1280]{2,1,0:T(8,128)(2,1)S(1)}, bf16[16,256,1280]{2,1,0:T(8,128)(2,1)S(1)}, bf16[5120,256]{1,0:T(8,128)(2,1)S(1)}, bf16[5120,256]{...) custom-call(s32[8,32]{1,0:T(8,128)} %bitcast.5, ...), custom_call_target="tpu_custom_call" | custom-call | flops 16106127360 | bytes 25165824 | tf_op jit(solution)/shard_map/first_inner/pallas_call | solution.py:519
  67.4 1.0 copy-done
  68.8 4.5 %first_edge.1 = (bf16[5120,256]{1,0:T(8,128)(2,1)S(1)}, bf16[5120,256]{1,0:T(8,128)(2,1)S(1)}, bf16[2,512,512]{2,1,0:T(8,128)(2,1)S(1)}, bf16[2,512,512]{2,1,0:T...) custom-call(s32[8,32]{1,0:T(8,128)} %bitcast.6, ...), custom_call_target="tpu_custom_call", output_to_operand_aliasing={{0}: (6, {}), {1}: (7, {})} | custom-call | flops 800000000 | bytes 6291456 | tf_op jit(solution)/shard_map/first_edge/pallas_call | solution.py:536
  73.3 3.6 %collective-permute-start.2 = (f32[512,256]{1,0:T(8,128)S(1)}, f32[512,256]{1,0:T(8,128)S(1)}, u32[]{:S(2)}, u32[]{:S(2)}) collective-permute-start(f32[512,256]{1,0:T(8,128)S(1)} %get-tuple-element.42), channel_id=1, source_target_pairs={{1,2},{3,4},{5,6},{7,8},{9,10},{11,12},{13,14},{15,16},{17,18},{19... | collective-permute-start | bytes 1572872 | tf_op jit(solution)/shard_map/ppermute | solution.py:477
  77.0 9.9 %inner.2 = (bf16[5120,256]{1,0:T(8,128)(2,1)S(1)}, bf16[5120,256]{1,0:T(8,128)(2,1)S(1)}, f32[1280,256]{1,0:T(8,128)S(1)}) custom-call(bf16[16,256,1280]{2,1,0:T(8,128)(2,1)S(1)} %get-tuple-element.36.rest_0_.hh, bf16[16,256,1280]{2,1,0:T(8,128)(2,1)S(1)} %get-tuple-element.37.rest_1_.hl, bf16[5120,256]{1,0:T(8,128)(2,1)S(1)} %get-tuple-element.44.vh.rest_2_.ph, ...), custom_call_target="tpu_custom_call" | custom-call | flops 8053063680 | bytes 1048576 | tf_op jit(solution)/shard_map/inner/pallas_call | solution.py:549
  86.9 1.8 edge.1
  88.7 7.0 %collective-permute-start.4 = (f32[512,256]{1,0:T(8,128)S(1)}, f32[512,256]{1,0:T(8,128)S(1)}, u32[]{:S(2)}, u32[]{:S(2)}) collective-permute-start(f32[512,256]{1,0:T(8,128)S(1)} %get-tuple-element.49), channel_id=1, source_target_pairs={{1,2},{3,4},{5,6},{7,8},{9,10},{11,12},{13,14},{15,16},{17,18},{19... | collective-permute-start | bytes 1572872 | tf_op jit(solution)/shard_map/ppermute | solution.py:477
  95.8 9.9 %inner.3 = (bf16[5120,256]{1,0:T(8,128)(2,1)S(1)}, bf16[5120,256]{1,0:T(8,128)(2,1)S(1)}, f32[1280,256]{1,0:T(8,128)S(1)}) custom-call(bf16[16,256,1280]{2,1,0:T(8,128)(2,1)S(1)} %get-tuple-element.36.rest_0_.hh, bf16[16,256,1280]{2,1,0:T(8,128)(2,1)S(1)} %get-tuple-element.37.rest_1_.hl, bf16[5120,256]{1,0:T(8,128)(2,1)S(1)} %get-tuple-element.51.vh, ...), custom_call_target="tpu_custom_call" | custom-call | flops 8053063680 | bytes 1048576 | tf_op jit(solution)/shard_map/inner/pallas_call | solution.py:549
  105.7 4.8 %last_edge_gram.1 = (bf16[5120,256]{1,0:T(8,128)(2,1)S(1)}, bf16[5120,256]{1,0:T(8,128)(2,1)S(1)}, f32[136,128]{1,0:T(8,128)S(1)}, f32[136,128]{1,0:T(8,128)S(1)}) custom-call(s32[8,32]{1,0:T(8,128)} %bitcast.8, bf16[2,512,512]{2,1,0:T(8,128)(2,1)S(1)} %get-tuple-element.40.xh, ...), custom_call_target="tpu_custom_call", output_to_operand_aliasing={{0}: (6, {}), {1}: (7, {})} | custom-call | flops 2000000000 | bytes 2097152 | tf_op jit(solution)/shard_map/last_edge_gram/pallas_call | solution.py:575
  111.1 0.9 collective-permute-done.6
  112.0 17.0 %collective-permute-start.9 = (f32[136,128]{1,0:T(8,128)S(1)}, f32[136,128]{1,0:T(8,128)S(1)}, u32[]{:S(2)}, u32[]{:S(2)}) collective-permute-start(f32[136,128]{1,0:T(8,128)S(1)} %add.30), channel_id=1, source_target_pairs={{0,96},{32,64},{64,32},{96,0},{1,97},{33,65},{65,33},{97,1},{2,98}... | collective-permute-start | bytes 208904 | tf_op jit(solution)/shard_map/ppermute | solution.py:485
  129.6 2.0 collective-permute-done.9
  131.6 2.0 collective-permute-done.8
  134.6 2.3 collective-permute-start.10
  137.0 1.9 collective-permute-done.12
  139.5 1.3 collective-permute-start.15
  140.8 2.0 collective-permute-start.13
  142.8 1.1 collective-permute-done.15
  143.9 1.5 collective-permute-done.14
  145.5 4.9 %collective-permute-start.16 = (f32[136,128]{1,0:T(8,128)S(1)}, f32[136,128]{1,0:T(8,128)S(1)}, u32[]{:S(2)}, u32[]{:S(2)}) collective-permute-start(f32[136,128]{1,0:T(8,128)S(1)} %add_add_fusion.mine), channel_id=1, source_target_pairs={{0,1},{1,0},{2,3},{3,2},{4,5},{5,4},{6,7},{7,6},{8,9},{9,8},{10,11... | collective-permute-start | bytes 208904 | tf_op jit(solution)/shard_map/ppermute | solution.py:590
  150.4 0.9 collective-permute-done.16.other
  151.3 117.8 %basis.1 = (f32[4096,256]{1,0:T(8,128)}, f32[256,256]{1,0:T(8,128)}) custom-call(s32[8,32]{1,0:T(8,128)} %bitcast.9, f32[136,128]{1,0:T(8,128)S(1)} %add_add_fusion.mine, f32[136,128]{1,0:T(8,128)S(1)} %collective-permute-done.16.other, bf16[5120,256]{1,0:T(8,128)(2,1)S(1)} %get-tuple-element.58.uh, bf16[5120,256]{1,0:T(8,128)(2,1)S(1)} %get-tuple-element.59.ul, ...), custom_call_target="tpu_custom_call" | custom-call | flops 2000000000 | bytes 4194304 | tf_op jit(solution)/shard_map/basis/pallas_call | solution.py:594
  (26 shorter events, 3.5 us)
Async XLA Ops:
  48.5 18.9 %collective-permute-start = (f32[2304,128]{1,0:T(8,128)}, f32[2304,128]{1,0:T(8,128)S(1)}, u32[]{:S(2)}, u32[]{:S(2)}) collective-permute-start(f32[2304,128]{1,0:T(8,128)} %get-tuple-element.31.sent_far), channel_id=1, source_target_pairs={{1,2},{3,4},{5,6},{7,8},{9,10},{11,12},{13,14},{15,16},{17,18},{19... | collective-permute-start | bytes 3538952 | tf_op jit(solution)/shard_map/ppermute | solution.py:477
  50.4 17.0 %collective-permute-start.1 = (f32[2304,128]{1,0:T(8,128)}, f32[2304,128]{1,0:T(8,128)S(1)}, u32[]{:S(2)}, u32[]{:S(2)}) collective-permute-start(f32[2304,128]{1,0:T(8,128)} %get-tuple-element.32.sent_near), channel_id=1, source_target_pairs={{0,1},{1,0},{2,3},{3,2},{4,5},{5,4},{6,7},{7,6},{8,9},{9,8},{10,11... | collective-permute-start | bytes 3538952 | tf_op jit(solution)/shard_map/ppermute | solution.py:478
  67.4 1.0 copy-start
  67.4 1.4 copy-start.1
  73.3 13.6 %collective-permute-start.2 = (f32[512,256]{1,0:T(8,128)S(1)}, f32[512,256]{1,0:T(8,128)S(1)}, u32[]{:S(2)}, u32[]{:S(2)}) collective-permute-start(f32[512,256]{1,0:T(8,128)S(1)} %get-tuple-element.42), channel_id=1, source_target_pairs={{1,2},{3,4},{5,6},{7,8},{9,10},{11,12},{13,14},{15,16},{17,18},{19... | collective-permute-start | bytes 1572872 | tf_op jit(solution)/shard_map/ppermute | solution.py:477
  76.9 10.0 %collective-permute-start.3 = (f32[512,256]{1,0:T(8,128)S(1)}, f32[512,256]{1,0:T(8,128)S(1)}, u32[]{:S(2)}, u32[]{:S(2)}) collective-permute-start(f32[512,256]{1,0:T(8,128)S(1)} %get-tuple-element.43), channel_id=1, source_target_pairs={{0,1},{1,0},{2,3},{3,2},{4,5},{5,4},{6,7},{7,6},{8,9},{9,8},{10,11... | collective-permute-start | bytes 1572872 | tf_op jit(solution)/shard_map/ppermute | solution.py:478
  88.7 17.0 %collective-permute-start.4 = (f32[512,256]{1,0:T(8,128)S(1)}, f32[512,256]{1,0:T(8,128)S(1)}, u32[]{:S(2)}, u32[]{:S(2)}) collective-permute-start(f32[512,256]{1,0:T(8,128)S(1)} %get-tuple-element.49), channel_id=1, source_target_pairs={{1,2},{3,4},{5,6},{7,8},{9,10},{11,12},{13,14},{15,16},{17,18},{19... | collective-permute-start | bytes 1572872 | tf_op jit(solution)/shard_map/ppermute | solution.py:477
  95.7 10.0 %collective-permute-start.5 = (f32[512,256]{1,0:T(8,128)S(1)}, f32[512,256]{1,0:T(8,128)S(1)}, u32[]{:S(2)}, u32[]{:S(2)}) collective-permute-start(f32[512,256]{1,0:T(8,128)S(1)} %get-tuple-element.50), channel_id=1, source_target_pairs={{0,1},{1,0},{2,3},{3,2},{4,5},{5,4},{6,7},{7,6},{8,9},{9,8},{10,11... | collective-permute-start | bytes 1572872 | tf_op jit(solution)/shard_map/ppermute | solution.py:478
  110.5 1.5 collective-permute-start.6
  112.0 19.7 %collective-permute-start.9 = (f32[136,128]{1,0:T(8,128)S(1)}, f32[136,128]{1,0:T(8,128)S(1)}, u32[]{:S(2)}, u32[]{:S(2)}) collective-permute-start(f32[136,128]{1,0:T(8,128)S(1)} %add.30), channel_id=1, source_target_pairs={{0,96},{32,64},{64,32},{96,0},{1,97},{33,65},{65,33},{97,1},{2,98}... | collective-permute-start | bytes 208904 | tf_op jit(solution)/shard_map/ppermute | solution.py:485
  129.0 4.7 %collective-permute-start.8 = (f32[136,128]{1,0:T(8,128)S(1)}, f32[136,128]{1,0:T(8,128)S(1)}, u32[]{:S(2)}, u32[]{:S(2)}) collective-permute-start(f32[136,128]{1,0:T(8,128)S(1)} %add.30), channel_id=1, source_target_pairs={{0,64},{32,96},{64,0},{96,32},{1,65},{33,97},{65,1},{97,33},{2,66}... | collective-permute-start | bytes 208904 | tf_op jit(solution)/shard_map/ppermute | solution.py:485
  129.1 4.5 %collective-permute-start.7 = (f32[136,128]{1,0:T(8,128)S(1)}, f32[136,128]{1,0:T(8,128)S(1)}, u32[]{:S(2)}, u32[]{:S(2)}) collective-permute-start(f32[136,128]{1,0:T(8,128)S(1)} %add.30), channel_id=1, source_target_pairs={{0,32},{32,0},{64,96},{96,64},{1,33},{33,1},{65,97},{97,65},{2,34}... | collective-permute-start | bytes 208904 | tf_op jit(solution)/shard_map/ppermute | solution.py:485
  133.7 5.2 %collective-permute-start.12 = (f32[136,128]{1,0:T(8,128)S(1)}, f32[136,128]{1,0:T(8,128)S(1)}, u32[]{:S(2)}, u32[]{:S(2)}) collective-permute-start(f32[136,128]{1,0:T(8,128)S(1)} %add_add_fusion.2), channel_id=1, source_target_pairs={{0,24},{8,16},{16,8},{24,0},{1,25},{9,17},{17,9},{25,1},{2,26},{10... | collective-permute-start | bytes 208904 | tf_op jit(solution)/shard_map/ppermute | solution.py:485
  133.8 5.1 %collective-permute-start.11 = (f32[136,128]{1,0:T(8,128)S(1)}, f32[136,128]{1,0:T(8,128)S(1)}, u32[]{:S(2)}, u32[]{:S(2)}) collective-permute-start(f32[136,128]{1,0:T(8,128)S(1)} %add_add_fusion.2), channel_id=1, source_target_pairs={{0,16},{8,24},{16,0},{24,8},{1,17},{9,25},{17,1},{25,9},{2,18},{10... | collective-permute-start | bytes 208904 | tf_op jit(solution)/shard_map/ppermute | solution.py:485
  134.6 4.8 %collective-permute-start.10 = (f32[136,128]{1,0:T(8,128)S(1)}, f32[136,128]{1,0:T(8,128)S(1)}, u32[]{:S(2)}, u32[]{:S(2)}) collective-permute-start(f32[136,128]{1,0:T(8,128)S(1)} %add_add_fusion.2), channel_id=1, source_target_pairs={{0,8},{8,0},{16,24},{24,16},{1,9},{9,1},{17,25},{25,17},{2,10},{10... | collective-permute-start | bytes 208904 | tf_op jit(solution)/shard_map/ppermute | solution.py:485
  139.5 4.5 %collective-permute-start.15 = (f32[136,128]{1,0:T(8,128)S(1)}, f32[136,128]{1,0:T(8,128)S(1)}, u32[]{:S(2)}, u32[]{:S(2)}) collective-permute-start(f32[136,128]{1,0:T(8,128)S(1)} %add_add_fusion.1), channel_id=1, source_target_pairs={{0,6},{2,4},{4,2},{6,0},{1,7},{3,5},{5,3},{7,1},{8,14},{10,12},{12... | collective-permute-start | bytes 208904 | tf_op jit(solution)/shard_map/ppermute | solution.py:485
  140.8 4.7 %collective-permute-start.14 = (f32[136,128]{1,0:T(8,128)S(1)}, f32[136,128]{1,0:T(8,128)S(1)}, u32[]{:S(2)}, u32[]{:S(2)}) collective-permute-start(f32[136,128]{1,0:T(8,128)S(1)} %add_add_fusion.1), channel_id=1, source_target_pairs={{0,4},{2,6},{4,0},{6,2},{1,5},{3,7},{5,1},{7,3},{8,12},{10,14},{12... | collective-permute-start | bytes 208904 | tf_op jit(solution)/shard_map/ppermute | solution.py:485
  140.8 4.7 %collective-permute-start.13 = (f32[136,128]{1,0:T(8,128)S(1)}, f32[136,128]{1,0:T(8,128)S(1)}, u32[]{:S(2)}, u32[]{:S(2)}) collective-permute-start(f32[136,128]{1,0:T(8,128)S(1)} %add_add_fusion.1), channel_id=1, source_target_pairs={{0,2},{2,0},{4,6},{6,4},{1,3},{3,1},{5,7},{7,5},{8,10},{10,8},{12,... | collective-permute-start | bytes 208904 | tf_op jit(solution)/shard_map/ppermute | solution.py:485
  145.5 5.8 %collective-permute-start.16 = (f32[136,128]{1,0:T(8,128)S(1)}, f32[136,128]{1,0:T(8,128)S(1)}, u32[]{:S(2)}, u32[]{:S(2)}) collective-permute-start(f32[136,128]{1,0:T(8,128)S(1)} %add_add_fusion.mine), channel_id=1, source_target_pairs={{0,1},{1,0},{2,3},{3,2},{4,5},{5,4},{6,7},{7,6},{8,9},{9,8},{10,11... | collective-permute-start | bytes 208904 | tf_op jit(solution)/shard_map/ppermute | solution.py:590

commit v2 on v1

--- a/solution.py
+++ b/solution.py
@@ -14,12 +14,13 @@
 WIDE = 10 * B
 EDGE = REACH * B
 LOCAL = ROWS * B
-EXT = LOCAL + 2 * EDGE
 DEAD = ROWS * SLOTS
 TABLE = (ROWS + 10) * 16
-RING = 16
-VRING = 6
+RING = 24
+VRING = 8
+GROUPS = ((0, 1), (2, 3, 4, 5), (6, 7, 8, 9), (10, 11, 12, 13), (14, 15))
 KEPT = 4
+CHUNK = 1024
 PAIRS_PREV = [(r, o) for r in range(4) for o in range(-4, 0) if r + o < 0]
 PAIRS_NEXT = [(r, o) for r in range(28, 32) for o in range(1, 5) if r + o > 31]
 PACKED = 10 * B + 2 * EDGE
@@ -119,26 +120,28 @@
         fill(swap_near, swap_far)
 
 
+def window_of(p):
+    return max(0, (2 - p) * 2 * B), WIDE - max(0, (p - PANELS + 3) * 2 * B)
+
+
 def apply_panel(p, hh, hl, vh, vl):
-    window = pl.ds(pl.multiple_of(p * 2 * B, 2 * B), WIDE)
-    return dot(hh, vh[window, :]) + dot(hl, vh[window, :]) + dot(hh, vl[window, :])
+    left, right = window_of(p)
+    window = slice(p * 2 * B + left - EDGE, p * 2 * B + right - EDGE)
+    high, low = hh[p, :, left:right], hl[p, :, left:right]
+    return dot(high, vh[window, :]) + dot(low, vh[window, :]) + dot(high, vl[window, :])
 
 
 def store_rows(p, value, uh, ul, part):
-    at = rows(EDGE + p * 2 * B, 2 * B)
+    at = slice(p * 2 * B, (p + 1) * 2 * B)
     uh[at, :], ul[at, :] = split(value)
-    spare = jnp.where(p < 2, p, jnp.where(p >= PANELS - 2, p - PANELS + 4, 4))
-    part[rows(spare * 2 * B, 2 * B), :] = value
-
-
-def clear_pads(*refs):
-    for ref in refs:
-        ref[:EDGE, :] = jnp.zeros((EDGE, K), BF16)
-        ref[EXT - EDGE :, :] = jnp.zeros((EDGE, K), BF16)
+    if p < 2:
+        part[p * 2 * B : (p + 1) * 2 * B, :] = value
+    elif p >= PANELS - 2:
+        part[(p - PANELS + 4) * 2 * B : (p - PANELS + 5) * 2 * B, :] = value
 
 
 def first_kernel(
-    columns, counts, blocks, vectors, hh, hl, vh, vl, uh, ul, part, table, sbuf, vbuf, ah, al, bh, bl, ssem, vsem
+    columns, counts, blocks, vectors, hh, hl, vh, vl, uh, ul, part, table, sbuf, vbuf, ssem, vsem
 ):
     def block_copy(r):
         return pltpu.make_async_copy(
@@ -154,17 +157,14 @@
 
     def take_vectors(q):
         vector_copy(q).wait()
-        at = rows(EDGE + q * 2 * B, 2 * B)
+        at = rows(q * 2 * B, 2 * B)
         vh[at, :], vl[at, :] = split(vbuf[q % VRING])
 
-    for q in range(VRING):
-        block_copy(2 * q).start()
-        block_copy(2 * q + 1).start()
-        vector_copy(q).start()
-    for r in range(2 * VRING, RING):
+    for r in range(RING):
         block_copy(r).start()
+        if r % 2 and r // 2 < VRING:
+            vector_copy(r // 2).start()
     sbuf[RING * SLOTS] = jnp.zeros((B, B), F32)
-    clear_pads(vh, vl, uh, ul)
     first = columns[0, 0]
 
     def clear(r, _):
@@ -179,77 +179,53 @@
     lax.fori_loop(0, ROWS + 10, clear, 0)
     lax.fori_loop(0, ROWS, fill, 0)
 
-    def fetch(slot, inside=True):
-        return sbuf[jnp.where(inside & (slot < DEAD), slot % (RING * SLOTS), RING * SLOTS)]
-
-    def build(p, high, low):
+    def fetch(slot):
+        return sbuf[jnp.where(slot < DEAD, slot % (RING * SLOTS), RING * SLOTS)]
+
+    def build(p):
+        left, right = window_of(p)
         for h in range(2):
             i = 2 * p + h
             at = slice(h * B, h * B + B)
-            for c in range(10):
+            for c in range(left // B, right // B):
                 o = c - 4 - h
                 cols = slice(c * B, c * B + B)
                 if abs(o) > REACH:
                     parts = (jnp.zeros((B, B), BF16),) * 2
                 else:
-                    near = fetch(table[place(i, o)], (i + o >= 0) & (i + o < ROWS))
-                    far = fetch(table[place(i + o, -o)])
-                    parts = split(near + far.T)
-                high[at, cols], low[at, cols] = parts
+                    parts = split(fetch(table[place(i, o)]) + fetch(table[place(i + o, -o)]).T)
                 hh[p, at, cols], hl[p, at, cols] = parts
 
-    def ready(p):
-        @pl.when(p < PANELS - 2)
-        def _():
-            block_copy(2 * p + 4).wait()
-            block_copy(2 * p + 5).wait()
-            take_vectors(p + 2)
-
-            @pl.when(p + 2 + VRING < PANELS)
-            def _():
-                vector_copy(p + 2 + VRING).start()
-
-    def refill(p):
-        @pl.when((p >= 3) & (p < PANELS - 5))
-        def _():
-            block_copy(2 * p + 10).start()
-            block_copy(2 * p + 11).start()
-
-    for r in range(REACH):
-        block_copy(r).wait()
-    for q in range(2):
-        take_vectors(q)
-        vector_copy(q + VRING).start()
-    ready(0)
-    build(0, ah, al)
-
-    def step(t, _):
-        p = 2 * t
-        refill(p)
-        refill(p + 1)
-        ready(p + 1)
-        ready(p + 2)
-        first_half = 0.5 * apply_panel(p, ah[...], al[...], vh, vl)
-        build(p + 1, bh, bl)
-        store_rows(p, first_half, uh, ul, part)
-        second_half = 0.5 * apply_panel(p + 1, bh[...], bl[...], vh, vl)
-        build(jnp.minimum(p + 2, PANELS - 1), ah, al)
-        store_rows(p + 1, second_half, uh, ul, part)
-        return 0
-
-    lax.fori_loop(0, PANELS // 2, step, 0)
+    rows_in = vectors_in = 0
+    rows_out, vectors_out = RING, VRING
+    before = ()
+    for group in GROUPS + ((),):
+        if group:
+            while rows_out < min(ROWS, RING + 2 * group[0] - REACH):
+                block_copy(rows_out).start()
+                rows_out += 1
+            while rows_in < min(ROWS, 2 * group[-1] + 6):
+                block_copy(rows_in).wait()
+                rows_in += 1
+            while vectors_in < min(PANELS, group[-1] + 3):
+                take_vectors(vectors_in)
+                vectors_in += 1
+            while vectors_out < min(PANELS, VRING + vectors_in):
+                vector_copy(vectors_out).start()
+                vectors_out += 1
+        for k in range(max(len(group), len(before))):
+            if k < len(group):
+                build(group[k])
+            if k < len(before):
+                store_rows(before[k], 0.5 * apply_panel(before[k], hh, hl, vh, vl), uh, ul, part)
+        before = group
 
 
 def inner_kernel(hh, hl, vh, vl, ph, pr, uh, ul, part):
-    clear_pads(uh, ul)
-
-    def step(p, _):
-        at = rows(EDGE + p * 2 * B, 2 * B)
+    for p in range(PANELS):
+        at = slice(p * 2 * B, (p + 1) * 2 * B)
         prior = ph[at, :].astype(F32) + pr[at, :].astype(F32)
-        store_rows(p, apply_panel(p, hh[p], hl[p], vh, vl) - prior, uh, ul, part)
-        return 0
-
-    lax.fori_loop(0, PANELS, step, 0, unroll=2)
+        store_rows(p, apply_panel(p, hh, hl, vh, vl) - prior, uh, ul, part)
 
 
 def cross(xh, xl, side, halo_high, halo_low):
@@ -257,57 +233,46 @@
 
 
 def write_edge(side, value, uh, ul):
-    start = EDGE if side == 0 else LOCAL
+    start = 0 if side == 0 else LOCAL - EDGE
     uh[start : start + EDGE, :], ul[start : start + EDGE, :] = split(value)
 
 
 def first_edge_kernel(
     columns, sent_far, sent_near, got_far, got_near, part, uh_in, ul_in, *rest
 ):
-    uh, ul, xh, xl, far, near, own, got, sems = rest[KEPT:]
+    uh, ul, xh, xl, far, near = rest[KEPT:]
     del uh_in, ul_in
     even = even_core(columns)
 
-    def fetch(refs):
-        moves = [
-            pltpu.make_async_copy(ref, place_, sems.at[k])
-            for k, (ref, place_) in enumerate(zip(refs, (own.at[0], own.at[1], got.at[0], got.at[1])))
-        ]
-        for move in moves:
-            move.start()
-        for move in moves:
-            move.wait()
-
-    @pl.when(even)
-    def _():
-        fetch((sent_far, sent_near, got_far, got_near))
-
-    @pl.when(jnp.logical_not(even))
-    def _():
-        fetch((sent_near, sent_far, got_near, got_far))
+    def own(side, at):
+        a, b = sent_far[at, :], sent_near[at, :]
+        return jnp.where(even, a, b) if side == 0 else jnp.where(even, b, a)
+
+    def got(side, at):
+        a, b = got_far[at, :], got_near[at, :]
+        return jnp.where(even, a, b) if side == 0 else jnp.where(even, b, a)
 
     zero = jnp.zeros((B, B), BF16)
     for r in range(REACH):
         for c in range(REACH):
             at, cols = slice(r * B, r * B + B), slice(c * B, c * B + B)
-            if c >= r:
-                a = PAIRS_PREV.index((r, c - 4 - r)) * B
-                b = PAIRS_NEXT.index((28 + c, 4 + r - c)) * B
-                value = own[0, a : a + B, :] + got[0, b : b + B, :].T
-                xh[0, at, cols], xl[0, at, cols] = split(value)
-            else:
-                xh[0, at, cols], xl[0, at, cols] = zero, zero
-            if c <= r:
-                a = PAIRS_NEXT.index((28 + r, 4 + c - r)) * B
-                b = PAIRS_PREV.index((c, r - c - 4)) * B
-                value = own[1, a : a + B, :] + got[1, b : b + B, :].T
-                xh[1, at, cols], xl[1, at, cols] = split(value)
-            else:
-                xh[1, at, cols], xl[1, at, cols] = zero, zero
+            for side in range(2):
+                if (c >= r) if side == 0 else (c <= r):
+                    if side == 0:
+                        a = PAIRS_PREV.index((r, c - 4 - r)) * B
+                        b = PAIRS_NEXT.index((28 + c, 4 + r - c)) * B
+                    else:
+                        a = PAIRS_NEXT.index((28 + r, 4 + c - r)) * B
+                        b = PAIRS_PREV.index((c, r - c - 4)) * B
+                    parts = split(own(side, slice(a, a + B)) + got(side, slice(b, b + B)).T)
+                else:
+                    parts = (zero, zero)
+                xh[side, at, cols], xl[side, at, cols] = parts
     values = []
     for side in range(2):
         halves = [
-            split(got[side, 10 * B + half * EDGE : 10 * B + (half + 1) * EDGE, :]) for half in range(2)
+            split(got(side, slice(10 * B + half * EDGE, 10 * B + (half + 1) * EDGE)))
+            for half in range(2)
         ]
         high = jnp.concatenate([halves[0][0], halves[1][0]], axis=1)
         low = jnp.concatenate([halves[0][1], halves[1][1]], axis=1)
@@ -345,16 +310,9 @@
     even, _ = finish_edges(columns, xh, xl, got_far, got_near, part, uh, ul)
     over = (((0,), (0,)), ((), ()))
 
-    def step(q, totals):
-        at = rows(EDGE + q * 512, 512)
-        high, low = uh[at, :], ul[at, :]
-        return (
-            totals[0] + lax.dot_general(high, high, over, preferred_element_type=F32),
-            totals[1] + lax.dot_general(high, low, over, preferred_element_type=F32),
-        )
-
-    zero = jnp.zeros((K, K), F32)
-    main, mixed = lax.fori_loop(0, LOCAL // 512, step, (zero, zero))
+    high, low = uh[...], ul[...]
+    main = lax.dot_general(high, high, over, preferred_element_type=F32)
+    mixed = lax.dot_general(high, low, over, preferred_element_type=F32)
     total = main + mixed + mixed.T
     r = lax.broadcasted_iota(jnp.int32, (B, B), 0)
     c = lax.broadcasted_iota(jnp.int32, (B, B), 1)
@@ -372,6 +330,15 @@
     return lax.dot_general(
         a, b, over, precision=lax.Precision.HIGHEST, preferred_element_type=F32
     )
+
+
+def close(a, b, over=(((1,), (0,)), ((), ()))):
+    (ah, al), (bh, bl) = split(a), split(b)
+
+    def product(x, y):
+        return lax.dot_general(x, y, over, preferred_element_type=F32)
+
+    return product(ah, bh) + (product(ah, bl) + product(al, bh))
 
 
 def basis_kernel(columns, mine, other, uh, ul, scale, basis, factor, work, upper, inverse, out, sems):
@@ -406,20 +373,20 @@
     left = (((0,), (0,)), ((), ()))
 
     def more(state):
-        return (state[0] > 1e-8) & (state[0] < 4.0) & (state[1] < 12)
+        return (state[0] > 1e-6) & (state[0] < 4.0) & (state[1] < 12)
 
     def newton(state):
         _, count, y = state
-        e = precise(y, precise(scaled, y), left) - eye
-        return (jnp.sum(e * e), count + 1, y - precise(y, half_upper(e)))
+        e = close(y, close(scaled, y), left) - eye
+        return (jnp.sum(e * e), count + 1, y - close(y, half_upper(e)))
 
     size, _, y = lax.while_loop(more, newton, (jnp.sum(gap * gap), 0, eye - half_upper(gap)))
-    settled = (size <= 1e-8) & (jnp.min(jnp.where(r == c, y, 1.0)) > 0.0)
+    settled = (size <= 1e-6) & (jnp.min(jnp.where(r == c, y, 1.0)) > 0.0)
 
     @pl.when(settled)
     def _():
         inverse[...] = y
-        full = precise(y, scaled, left)
+        full = close(y, scaled, left)
         upper[...] = jnp.where(c >= r, full, 0.0)
 
     @pl.when(jnp.logical_not(settled))
@@ -457,17 +424,17 @@
     wh, wl = split(inverse[...] * (col_s * root))
 
     def out_copy(q):
-        at = rows(q * 256, 256)
+        at = rows(q * CHUNK, CHUNK)
         return pltpu.make_async_copy(out.at[at, :], basis.at[at, :], sems.at[q])
 
     def step(q, _):
-        at = rows(EDGE + q * 256, 256)
-        out[rows(q * 256, 256), :] = dot(uh[at, :], wh) + dot(ul[at, :], wh) + dot(uh[at, :], wl)
+        at = rows(q * CHUNK, CHUNK)
+        out[at, :] = dot(uh[at, :], wh) + dot(ul[at, :], wh) + dot(uh[at, :], wl)
         out_copy(q).start()
         return 0
 
-    lax.fori_loop(0, LOCAL // 256, step, 0, unroll=2)
-    for q in range(LOCAL // 256):
+    lax.fori_loop(0, LOCAL // CHUNK, step, 0)
+    for q in range(LOCAL // CHUNK):
         out_copy(q).wait()
 
 
@@ -492,12 +459,12 @@
         pltpu.with_memory_space_constraint(x, pltpu.HBM)
         for x in (blocks.reshape(DEAD, B, B), start_vectors, counts, columns.T)
     )
-    packed = pltpu.HBM((PACKED, B), F32)
+    packed = pltpu.VMEM((PACKED, B), F32)
     sent = pl.pallas_call(
         pack_kernel,
         out_shape=(packed, packed),
         in_specs=(SM, SM, HB, HB),
-        out_specs=(HB, HB),
+        out_specs=(VM, VM),
         scratch_shapes=[
             pltpu.SMEM((TABLE + 1,), jnp.int32),
             pltpu.VMEM((B, B), F32),
@@ -507,12 +474,11 @@
         cost_estimate=cost(0, 2 * 2 * PACKED * B * 4),
         name="pack_edges",
     )(columns, counts, flat, start_vectors)
-    sent = [pltpu.with_memory_space_constraint(x, pltpu.HBM) for x in sent]
     got = swap_pairs(*sent)
 
     wide = pltpu.VMEM((PANELS, 2 * B, WIDE), BF16)
-    slab = pltpu.VMEM((EXT, K), BF16)
-    partial = pltpu.VMEM((10 * B, K), F32)
+    slab = pltpu.VMEM((LOCAL, K), BF16)
+    partial = pltpu.VMEM((2 * EDGE, K), F32)
     crossing = pltpu.VMEM((2, EDGE, EDGE), BF16)
     edge = jax.ShapeDtypeStruct((EDGE, K), F32)
     flops = 3 * 2 * PANELS * 2 * B * WIDE * K
@@ -526,9 +492,8 @@
             pltpu.VMEM((RING * SLOTS + 1, B, B), F32),
             pltpu.VMEM((VRING, 2 * B, K), F32),
         ]
-        + [pltpu.VMEM((2 * B, WIDE), BF16)] * 4
         + [pltpu.SemaphoreType.DMA((RING,)), pltpu.SemaphoreType.DMA((VRING,))],
-        compiler_params=params(14),
+        compiler_params=params(16),
         cost_estimate=cost(flops * 2, 24 * 2**20),
         name="first_inner",
     )(columns, counts, flat, start_vectors)
@@ -536,11 +501,10 @@
     uh, ul, xh, xl, far, near = pl.pallas_call(
         first_edge_kernel,
         out_shape=(slab, slab, crossing, crossing, edge, edge),
-        in_specs=(SM,) + (HB,) * 4 + (VM,) * (3 + KEPT),
+        in_specs=(SM,) + (VM,) * (7 + KEPT),
         out_specs=(VM,) * 6,
         input_output_aliases={6: 0, 7: 1},
-        scratch_shapes=[pltpu.VMEM((2, PACKED, B), F32)] * 2 + [pltpu.SemaphoreType.DMA((4,))],
-        compiler_params=params(8),
+        compiler_params=params(4),
         cost_estimate=cost(8e8, 6 * 2**20),
         name="first_edge",
     )(columns, *sent, *got, part, uh, ul, hh, hl, vh, vl)
@@ -597,8 +561,8 @@
         in_specs=(SM, VM, VM, VM, VM, SM),
         out_specs=(HB, VM),
         scratch_shapes=[pltpu.VMEM((K, K), F32)] * 3
-        + [pltpu.VMEM((LOCAL, K), F32), pltpu.SemaphoreType.DMA((LOCAL // 256,))],
-        compiler_params=params(10),
+        + [pltpu.VMEM((LOCAL, K), F32), pltpu.SemaphoreType.DMA((LOCAL // CHUNK,))],
+        compiler_params=params(12),
         cost_estimate=cost(2e9, 4 * 2**20),
         name="basis",
     )(columns, mine, other, fh, fl, scale)

time: 271 us -> 210 us (0.77)
  Pallas kernels: 213 us -> 158 us
  starting transfers between devices: 42.6 us -> 38.4 us
    pallas_call x1, Pallas kernels: 47.9 us -> 2.95 us  [body(): pl.pallas_call(pack_kernel, out_shape=(packed, packed), in_specs=(SM, SM,...]
    pallas_call x2, Pallas kernels: 19.7 us -> 15.4 us  [inner(): pl.pallas_call(inner_kernel, out_shape=(slab, slab, partial), in_specs=(V...]
    ppermute x9, starting transfers between devices: 24.3 us -> 20.5 us  [group_sum(): lax.ppermute(value, axis, [(i, i ^ k) for i in range(count)])]
  transfers between devices with their start and end apart: 17 -> 17, of which waited for: 8 -> 8; matrix products, arithmetic and copies ran while one was open for 0% -> 0% of each run, Pallas kernels for 14% -> 15%
where the time goes in v2:
time: 210 us
  Pallas kernels  158 us (75%)
  starting transfers between devices  38.4 us (18%)
  waiting for transfers between devices  12.3 us (6%)
    pallas_call x1, Pallas kernels, body(): pl.pallas_call(basis_kernel, out_shape=(jax.ShapeDtypeStruct((LOCAL, K),...  117 us
    ppermute x9, starting transfers between devices, group_sum(): lax.ppermute(value, axis, [(i, i ^ k) for i in range(count)])  20.5 us
    pallas_call x1, Pallas kernels, body(): pl.pallas_call(first_kernel, out_shape=(wide, wide, slab, slab, slab, sla...  15.5 us
    pallas_call x2, Pallas kernels, inner(): pl.pallas_call(inner_kernel, out_shape=(slab, slab, partial), in_specs=(V...  15.4 us
    ppermute x3, starting transfers between devices, swap_pairs(): got_far = lax.ppermute(far, ALL, pairs + [(j, i) for i, j in pairs])  12.5 us
    ppermute x9, waiting for transfers between devices, group_sum(): lax.ppermute(value, axis, [(i, i ^ k) for i in range(count)])  10.4 us
    ppermute x1, starting transfers between devices, body(): other = lax.ppermute(mine, 'c', swap)  4.41 us
  transfers between devices with their start and end apart: 17, of which 8 were waited for; matrix products, arithmetic and copies ran while one was open for 0% of the time, Pallas kernels for 15%

profile of v2, /device:TPU:1, one launch (start us, length us, event | category | flops | bytes accessed | tf_op | source)
XLA Modules:
  0.0 209.7 jit_solution(13578209159141936067)
XLA Ops:
  0.6 2.9 %pack_edges.1 = (f32[2304,128]{1,0:T(8,128)S(1)}, f32[2304,128]{1,0:T(8,128)S(1)}) custom-call(s32[8,32]{1,0:T(8,128)} %bitcast.4, s32[32]{0:T(128)} %counts.3, f32[256,128,128]{2,1,0:T(8,128)} %bitcast.2, f32[4096,256]{1,0:T(8,128)} %vectors.3), custom_call_target="tpu_custom_call" | custom-call | bytes 4718592 | tf_op jit(solution)/shard_map/pack_edges/pallas_call | solution.py:463
  3.6 5.3 %collective-permute-start = (f32[2304,128]{1,0:T(8,128)S(1)}, f32[2304,128]{1,0:T(8,128)S(1)}, u32[]{:S(2)}, u32[]{:S(2)}) collective-permute-start(f32[2304,128]{1,0:T(8,128)S(1)} %get-tuple-element.31.sent_far), channel_id=1, source_target_pairs={{1,2},{3,4},{5,6},{7,8},{9,10},{11,12},{13,14},{15,16},{17,18},{19... | collective-permute-start | bytes 3538952 | tf_op jit(solution)/shard_map/ppermute | solution.py:444
  9.0 15.5 %first_inner.1 = (bf16[16,256,1280]{2,1,0:T(8,128)(2,1)S(1)}, bf16[16,256,1280]{2,1,0:T(8,128)(2,1)S(1)}, bf16[4096,256]{1,0:T(8,128)(2,1)S(1)}, bf16[4096,256]{...) custom-call(s32[8,32]{1,0:T(8,128)} %bitcast.5, ...), custom_call_target="tpu_custom_call" | custom-call | flops 16106127360 | bytes 25165824 | tf_op jit(solution)/shard_map/first_inner/pallas_call | solution.py:485
  24.5 2.2 %first_edge.1 = (bf16[4096,256]{1,0:T(8,128)(2,1)S(1)}, bf16[4096,256]{1,0:T(8,128)(2,1)S(1)}, bf16[2,512,512]{2,1,0:T(8,128)(2,1)S(1)}, bf16[2,512,512]{2,1,0:T...) custom-call(s32[8,32]{1,0:T(8,128)} %bitcast.6, ...), custom_call_target="tpu_custom_call", output_to_operand_aliasing={{0}: (6, {}), {1}: (7, {})} | custom-call | flops 800000000 | bytes 6291456 | tf_op jit(solution)/shard_map/first_edge/pallas_call | solution.py:501
  26.7 3.5 %collective-permute-start.2 = (f32[512,256]{1,0:T(8,128)S(1)}, f32[512,256]{1,0:T(8,128)S(1)}, u32[]{:S(2)}, u32[]{:S(2)}) collective-permute-start(f32[512,256]{1,0:T(8,128)S(1)} %get-tuple-element.42), channel_id=1, source_target_pairs={{1,2},{3,4},{5,6},{7,8},{9,10},{11,12},{13,14},{15,16},{17,18},{19... | collective-permute-start | bytes 1572872 | tf_op jit(solution)/shard_map/ppermute | solution.py:444
  30.5 7.7 %inner.2 = (bf16[4096,256]{1,0:T(8,128)(2,1)S(1)}, bf16[4096,256]{1,0:T(8,128)(2,1)S(1)}, f32[1024,256]{1,0:T(8,128)S(1)}) custom-call(bf16[16,256,1280]{2,1,0:T(8,128)(2,1)S(1)} %get-tuple-element.36.rest_0_.hh, bf16[16,256,1280]{2,1,0:T(8,128)(2,1)S(1)} %get-tuple-element.37.rest_1_.hl, bf16[4096,256]{1,0:T(8,128)(2,1)S(1)} %get-tuple-element.44.vh.rest_2_.ph, ...), custom_call_target="tpu_custom_call" | custom-call | flops 8053063680 | bytes 1048576 | tf_op jit(solution)/shard_map/inner/pallas_call | solution.py:513
  38.2 1.8 edge.1
  40.0 3.7 %collective-permute-start.4 = (f32[512,256]{1,0:T(8,128)S(1)}, f32[512,256]{1,0:T(8,128)S(1)}, u32[]{:S(2)}, u32[]{:S(2)}) collective-permute-start(f32[512,256]{1,0:T(8,128)S(1)} %get-tuple-element.49), channel_id=1, source_target_pairs={{1,2},{3,4},{5,6},{7,8},{9,10},{11,12},{13,14},{15,16},{17,18},{19... | collective-permute-start | bytes 1572872 | tf_op jit(solution)/shard_map/ppermute | solution.py:444
  43.9 7.7 %inner.3 = (bf16[4096,256]{1,0:T(8,128)(2,1)S(1)}, bf16[4096,256]{1,0:T(8,128)(2,1)S(1)}, f32[1024,256]{1,0:T(8,128)S(1)}) custom-call(bf16[16,256,1280]{2,1,0:T(8,128)(2,1)S(1)} %get-tuple-element.36.rest_0_.hh, bf16[16,256,1280]{2,1,0:T(8,128)(2,1)S(1)} %get-tuple-element.37.rest_1_.hl, bf16[4096,256]{1,0:T(8,128)(2,1)S(1)} %get-tuple-element.51.vh, ...), custom_call_target="tpu_custom_call" | custom-call | flops 8053063680 | bytes 1048576 | tf_op jit(solution)/shard_map/inner/pallas_call | solution.py:513
  51.6 3.1 %last_edge_gram.1 = (bf16[4096,256]{1,0:T(8,128)(2,1)S(1)}, bf16[4096,256]{1,0:T(8,128)(2,1)S(1)}, f32[136,128]{1,0:T(8,128)S(1)}, f32[136,128]{1,0:T(8,128)S(1)}) custom-call(s32[8,32]{1,0:T(8,128)} %bitcast.8, bf16[2,512,512]{2,1,0:T(8,128)(2,1)S(1)} %get-tuple-element.40.xh, ...), custom_call_target="tpu_custom_call", output_to_operand_aliasing={{0}: (6, {}), {1}: (7, {})} | custom-call | flops 2000000000 | bytes 2097152 | tf_op jit(solution)/shard_map/last_edge_gram/pallas_call | solution.py:539
  54.7 0.6 collective-permute-start.6
  55.2 0.9 collective-permute-done.6
  56.2 12.8 %collective-permute-start.9 = (f32[136,128]{1,0:T(8,128)S(1)}, f32[136,128]{1,0:T(8,128)S(1)}, u32[]{:S(2)}, u32[]{:S(2)}) collective-permute-start(f32[136,128]{1,0:T(8,128)S(1)} %add.30), channel_id=1, source_target_pairs={{0,96},{32,64},{64,32},{96,0},{1,97},{33,65},{65,33},{97,1},{2,98}... | collective-permute-start | bytes 208904 | tf_op jit(solution)/shard_map/ppermute | solution.py:452
  69.6 2.0 collective-permute-done.9
  71.6 2.0 collective-permute-done.8
  73.8 3.1 %collective-permute-start.10 = (f32[136,128]{1,0:T(8,128)S(1)}, f32[136,128]{1,0:T(8,128)S(1)}, u32[]{:S(2)}, u32[]{:S(2)}) collective-permute-start(f32[136,128]{1,0:T(8,128)S(1)} %add_add_fusion.2), channel_id=1, source_target_pairs={{0,8},{8,0},{16,24},{24,16},{1,9},{9,1},{17,25},{25,17},{2,10},{10... | collective-permute-start | bytes 208904 | tf_op jit(solution)/shard_map/ppermute | solution.py:452
  77.0 1.9 collective-permute-done.12
  79.4 3.0 %collective-permute-start.15 = (f32[136,128]{1,0:T(8,128)S(1)}, f32[136,128]{1,0:T(8,128)S(1)}, u32[]{:S(2)}, u32[]{:S(2)}) collective-permute-start(f32[136,128]{1,0:T(8,128)S(1)} %add_add_fusion.1), channel_id=1, source_target_pairs={{0,6},{2,4},{4,2},{6,0},{1,7},{3,5},{5,3},{7,1},{8,14},{10,12},{12... | collective-permute-start | bytes 208904 | tf_op jit(solution)/shard_map/ppermute | solution.py:452
  82.4 0.7 collective-permute-start.13
  83.1 1.3 collective-permute-done.15
  84.4 2.7 %collective-permute-done.14 = f32[136,128]{1,0:T(8,128)S(1)} collective-permute-done((f32[136,128]{1,0:T(8,128)S(1)}, f32[136,128]{1,0:T(8,128)S(1)}, u32[]{:S(2)}, u32[]{:S(2)}) %collective-permute-start.14) | collective-permute-done | bytes 69664 | tf_op jit(solution)/shard_map/ppermute | solution.py:452
  87.1 4.4 %collective-permute-start.16 = (f32[136,128]{1,0:T(8,128)S(1)}, f32[136,128]{1,0:T(8,128)S(1)}, u32[]{:S(2)}, u32[]{:S(2)}) collective-permute-start(f32[136,128]{1,0:T(8,128)S(1)} %add_add_fusion.mine), channel_id=1, source_target_pairs={{0,1},{1,0},{2,3},{3,2},{4,5},{5,4},{6,7},{7,6},{8,9},{9,8},{10,11... | collective-permute-start | bytes 208904 | tf_op jit(solution)/shard_map/ppermute | solution.py:554
  91.5 0.9 collective-permute-done.16.other
  92.4 117.0 %basis.1 = (f32[4096,256]{1,0:T(8,128)}, f32[256,256]{1,0:T(8,128)}) custom-call(s32[8,32]{1,0:T(8,128)} %bitcast.9, f32[136,128]{1,0:T(8,128)S(1)} %add_add_fusion.mine, f32[136,128]{1,0:T(8,128)S(1)} %collective-permute-done.16.other, bf16[4096,256]{1,0:T(8,128)(2,1)S(1)} %get-tuple-element.58.uh, bf16[4096,256]{1,0:T(8,128)(2,1)S(1)} %get-tuple-element.59.ul, ...), custom_call_target="tpu_custom_call" | custom-call | flops 2000000000 | bytes 4194304 | tf_op jit(solution)/shard_map/basis/pallas_call | solution.py:558
  (22 shorter events, 1.9 us)
Async XLA Ops:
  3.6 20.9 %collective-permute-start = (f32[2304,128]{1,0:T(8,128)S(1)}, f32[2304,128]{1,0:T(8,128)S(1)}, u32[]{:S(2)}, u32[]{:S(2)}) collective-permute-start(f32[2304,128]{1,0:T(8,128)S(1)} %get-tuple-element.31.sent_far), channel_id=1, source_target_pairs={{1,2},{3,4},{5,6},{7,8},{9,10},{11,12},{13,14},{15,16},{17,18},{19... | collective-permute-start | bytes 3538952 | tf_op jit(solution)/shard_map/ppermute | solution.py:444
  8.9 15.6 %collective-permute-start.1 = (f32[2304,128]{1,0:T(8,128)S(1)}, f32[2304,128]{1,0:T(8,128)S(1)}, u32[]{:S(2)}, u32[]{:S(2)}) collective-permute-start(f32[2304,128]{1,0:T(8,128)S(1)} %get-tuple-element.32.sent_near), channel_id=1, source_target_pairs={{0,1},{1,0},{2,3},{3,2},{4,5},{5,4},{6,7},{7,6},{8,9},{9,8},{10,11... | collective-permute-start | bytes 3538952 | tf_op jit(solution)/shard_map/ppermute | solution.py:445
  26.7 11.5 %collective-permute-start.2 = (f32[512,256]{1,0:T(8,128)S(1)}, f32[512,256]{1,0:T(8,128)S(1)}, u32[]{:S(2)}, u32[]{:S(2)}) collective-permute-start(f32[512,256]{1,0:T(8,128)S(1)} %get-tuple-element.42), channel_id=1, source_target_pairs={{1,2},{3,4},{5,6},{7,8},{9,10},{11,12},{13,14},{15,16},{17,18},{19... | collective-permute-start | bytes 1572872 | tf_op jit(solution)/shard_map/ppermute | solution.py:444
  30.2 8.0 %collective-permute-start.3 = (f32[512,256]{1,0:T(8,128)S(1)}, f32[512,256]{1,0:T(8,128)S(1)}, u32[]{:S(2)}, u32[]{:S(2)}) collective-permute-start(f32[512,256]{1,0:T(8,128)S(1)} %get-tuple-element.43), channel_id=1, source_target_pairs={{0,1},{1,0},{2,3},{3,2},{4,5},{5,4},{6,7},{7,6},{8,9},{9,8},{10,11... | collective-permute-start | bytes 1572872 | tf_op jit(solution)/shard_map/ppermute | solution.py:445
  40.0 11.5 %collective-permute-start.4 = (f32[512,256]{1,0:T(8,128)S(1)}, f32[512,256]{1,0:T(8,128)S(1)}, u32[]{:S(2)}, u32[]{:S(2)}) collective-permute-start(f32[512,256]{1,0:T(8,128)S(1)} %get-tuple-element.49), channel_id=1, source_target_pairs={{1,2},{3,4},{5,6},{7,8},{9,10},{11,12},{13,14},{15,16},{17,18},{19... | collective-permute-start | bytes 1572872 | tf_op jit(solution)/shard_map/ppermute | solution.py:444
  43.8 7.8 %collective-permute-start.5 = (f32[512,256]{1,0:T(8,128)S(1)}, f32[512,256]{1,0:T(8,128)S(1)}, u32[]{:S(2)}, u32[]{:S(2)}) collective-permute-start(f32[512,256]{1,0:T(8,128)S(1)} %get-tuple-element.50), channel_id=1, source_target_pairs={{0,1},{1,0},{2,3},{3,2},{4,5},{5,4},{6,7},{7,6},{8,9},{9,8},{10,11... | collective-permute-start | bytes 1572872 | tf_op jit(solution)/shard_map/ppermute | solution.py:445
  54.7 1.5 collective-permute-start.6
  56.2 15.5 %collective-permute-start.9 = (f32[136,128]{1,0:T(8,128)S(1)}, f32[136,128]{1,0:T(8,128)S(1)}, u32[]{:S(2)}, u32[]{:S(2)}) collective-permute-start(f32[136,128]{1,0:T(8,128)S(1)} %add.30), channel_id=1, source_target_pairs={{0,96},{32,64},{64,32},{96,0},{1,97},{33,65},{65,33},{97,1},{2,98}... | collective-permute-start | bytes 208904 | tf_op jit(solution)/shard_map/ppermute | solution.py:452
  68.9 4.7 %collective-permute-start.8 = (f32[136,128]{1,0:T(8,128)S(1)}, f32[136,128]{1,0:T(8,128)S(1)}, u32[]{:S(2)}, u32[]{:S(2)}) collective-permute-start(f32[136,128]{1,0:T(8,128)S(1)} %add.30), channel_id=1, source_target_pairs={{0,64},{32,96},{64,0},{96,32},{1,65},{33,97},{65,1},{97,33},{2,66}... | collective-permute-start | bytes 208904 | tf_op jit(solution)/shard_map/ppermute | solution.py:452
  69.4 4.3 %collective-permute-start.7 = (f32[136,128]{1,0:T(8,128)S(1)}, f32[136,128]{1,0:T(8,128)S(1)}, u32[]{:S(2)}, u32[]{:S(2)}) collective-permute-start(f32[136,128]{1,0:T(8,128)S(1)} %add.30), channel_id=1, source_target_pairs={{0,32},{32,0},{64,96},{96,64},{1,33},{33,1},{65,97},{97,65},{2,34}... | collective-permute-start | bytes 208904 | tf_op jit(solution)/shard_map/ppermute | solution.py:452
  73.6 5.2 %collective-permute-start.12 = (f32[136,128]{1,0:T(8,128)S(1)}, f32[136,128]{1,0:T(8,128)S(1)}, u32[]{:S(2)}, u32[]{:S(2)}) collective-permute-start(f32[136,128]{1,0:T(8,128)S(1)} %add_add_fusion.2), channel_id=1, source_target_pairs={{0,24},{8,16},{16,8},{24,0},{1,25},{9,17},{17,9},{25,1},{2,26},{10... | collective-permute-start | bytes 208904 | tf_op jit(solution)/shard_map/ppermute | solution.py:452
  73.7 5.1 %collective-permute-start.11 = (f32[136,128]{1,0:T(8,128)S(1)}, f32[136,128]{1,0:T(8,128)S(1)}, u32[]{:S(2)}, u32[]{:S(2)}) collective-permute-start(f32[136,128]{1,0:T(8,128)S(1)} %add_add_fusion.2), channel_id=1, source_target_pairs={{0,16},{8,24},{16,0},{24,8},{1,17},{9,25},{17,1},{25,9},{2,18},{10... | collective-permute-start | bytes 208904 | tf_op jit(solution)/shard_map/ppermute | solution.py:452
  73.8 5.6 %collective-permute-start.10 = (f32[136,128]{1,0:T(8,128)S(1)}, f32[136,128]{1,0:T(8,128)S(1)}, u32[]{:S(2)}, u32[]{:S(2)}) collective-permute-start(f32[136,128]{1,0:T(8,128)S(1)} %add_add_fusion.2), channel_id=1, source_target_pairs={{0,8},{8,0},{16,24},{24,16},{1,9},{9,1},{17,25},{25,17},{2,10},{10... | collective-permute-start | bytes 208904 | tf_op jit(solution)/shard_map/ppermute | solution.py:452
  79.4 5.0 %collective-permute-start.15 = (f32[136,128]{1,0:T(8,128)S(1)}, f32[136,128]{1,0:T(8,128)S(1)}, u32[]{:S(2)}, u32[]{:S(2)}) collective-permute-start(f32[136,128]{1,0:T(8,128)S(1)} %add_add_fusion.1), channel_id=1, source_target_pairs={{0,6},{2,4},{4,2},{6,0},{1,7},{3,5},{5,3},{7,1},{8,14},{10,12},{12... | collective-permute-start | bytes 208904 | tf_op jit(solution)/shard_map/ppermute | solution.py:452
  82.4 4.7 %collective-permute-start.14 = (f32[136,128]{1,0:T(8,128)S(1)}, f32[136,128]{1,0:T(8,128)S(1)}, u32[]{:S(2)}, u32[]{:S(2)}) collective-permute-start(f32[136,128]{1,0:T(8,128)S(1)} %add_add_fusion.1), channel_id=1, source_target_pairs={{0,4},{2,6},{4,0},{6,2},{1,5},{3,7},{5,1},{7,3},{8,12},{10,14},{12... | collective-permute-start | bytes 208904 | tf_op jit(solution)/shard_map/ppermute | solution.py:452
  82.4 4.7 %collective-permute-start.13 = (f32[136,128]{1,0:T(8,128)S(1)}, f32[136,128]{1,0:T(8,128)S(1)}, u32[]{:S(2)}, u32[]{:S(2)}) collective-permute-start(f32[136,128]{1,0:T(8,128)S(1)} %add_add_fusion.1), channel_id=1, source_target_pairs={{0,2},{2,0},{4,6},{6,4},{1,3},{3,1},{5,7},{7,5},{8,10},{10,8},{12,... | collective-permute-start | bytes 208904 | tf_op jit(solution)/shard_map/ppermute | solution.py:452
  87.1 5.3 %collective-permute-start.16 = (f32[136,128]{1,0:T(8,128)S(1)}, f32[136,128]{1,0:T(8,128)S(1)}, u32[]{:S(2)}, u32[]{:S(2)}) collective-permute-start(f32[136,128]{1,0:T(8,128)S(1)} %add_add_fusion.mine), channel_id=1, source_target_pairs={{0,1},{1,0},{2,3},{3,2},{4,5},{5,4},{6,7},{7,6},{8,9},{9,8},{10,11... | collective-permute-start | bytes 208904 | tf_op jit(solution)/shard_map/ppermute | solution.py:554

commit v3 on v2

--- a/solution.py
+++ b/solution.py
@@ -20,7 +20,7 @@
 VRING = 8
 GROUPS = ((0, 1), (2, 3, 4, 5), (6, 7, 8, 9), (10, 11, 12, 13), (14, 15))
 KEPT = 4
-CHUNK = 1024
+CHUNK = 2048
 PAIRS_PREV = [(r, o) for r in range(4) for o in range(-4, 0) if r + o < 0]
 PAIRS_NEXT = [(r, o) for r in range(28, 32) for o in range(1, 5) if r + o > 31]
 PACKED = 10 * B + 2 * EDGE
@@ -143,12 +143,25 @@
 def first_kernel(
     columns, counts, blocks, vectors, hh, hl, vh, vl, uh, ul, part, table, sbuf, vbuf, ssem, vsem
 ):
-    def block_copy(r):
-        return pltpu.make_async_copy(
-            blocks.at[pl.ds(r * SLOTS, SLOTS)],
-            sbuf.at[rows((r % RING) * SLOTS, SLOTS)],
-            ssem.at[r % RING],
-        )
+    class block_copy:
+        def __init__(self, r):
+            self.more = counts[r] > SLOTS // 2
+            self.parts = [
+                pltpu.make_async_copy(
+                    blocks.at[pl.ds(r * SLOTS + k * 4, SLOTS // 2)],
+                    sbuf.at[pl.ds((r % RING) * SLOTS + k * 4, SLOTS // 2)],
+                    ssem.at[r % RING, k],
+                )
+                for k in range(2)
+            ]
+
+        def start(self):
+            self.parts[0].start()
+            pl.when(self.more)(self.parts[1].start)
+
+        def wait(self):
+            self.parts[0].wait()
+            pl.when(self.more)(self.parts[1].wait)
 
     def vector_copy(q):
         return pltpu.make_async_copy(
@@ -221,11 +234,22 @@
         before = group
 
 
-def inner_kernel(hh, hl, vh, vl, ph, pr, uh, ul, part):
+def inner_kernel(hh, hl, vh, vl, ph, pr, uh, ul, part, *gram):
     for p in range(PANELS):
         at = slice(p * 2 * B, (p + 1) * 2 * B)
         prior = ph[at, :].astype(F32) + pr[at, :].astype(F32)
         store_rows(p, apply_panel(p, hh, hl, vh, vl) - prior, uh, ul, part)
+    if gram:
+        gram[0][0], gram[0][1] = gram_parts(slice(EDGE, LOCAL - EDGE), uh, ul)
+
+
+def gram_parts(at, high, low):
+    over = (((0,), (0,)), ((), ()))
+    flipped = high[at, :]
+    return (
+        lax.dot_general(flipped, high[at, :], over, preferred_element_type=F32),
+        lax.dot_general(flipped, low[at, :], over, preferred_element_type=F32),
+    )
 
 
 def cross(xh, xl, side, halo_high, halo_low):
@@ -305,14 +329,12 @@
     send_edges(even, values, far, near)
 
 
-def last_edge_kernel(columns, xh, xl, got_far, got_near, part, uh_in, ul_in, uh, ul, mine, theirs):
+def last_edge_kernel(columns, xh, xl, got_far, got_near, part, uh_in, ul_in, inside, uh, ul, mine, theirs):
     del uh_in, ul_in
     even, _ = finish_edges(columns, xh, xl, got_far, got_near, part, uh, ul)
-    over = (((0,), (0,)), ((), ()))
-
-    high, low = uh[...], ul[...]
-    main = lax.dot_general(high, high, over, preferred_element_type=F32)
-    mixed = lax.dot_general(high, low, over, preferred_element_type=F32)
+    first = gram_parts(slice(0, EDGE), uh, ul)
+    last = gram_parts(slice(LOCAL - EDGE, LOCAL), uh, ul)
+    main, mixed = (inside[k] + (first[k] + last[k]) for k in range(2))
     total = main + mixed + mixed.T
     r = lax.broadcasted_iota(jnp.int32, (B, B), 0)
     c = lax.broadcasted_iota(jnp.int32, (B, B), 1)
@@ -372,16 +394,19 @@
 
     left = (((0,), (0,)), ((), ()))
 
+    def measured(y):
+        e = close(y, close(scaled, y), left) - eye
+        return jnp.sum(e * e), e, y
+
     def more(state):
-        return (state[0] > 1e-6) & (state[0] < 4.0) & (state[1] < 12)
+        return (state[0] > 1e-7) & (state[0] < 4.0) & (state[3] < 12)
 
     def newton(state):
-        _, count, y = state
-        e = close(y, close(scaled, y), left) - eye
-        return (jnp.sum(e * e), count + 1, y - close(y, half_upper(e)))
-
-    size, _, y = lax.while_loop(more, newton, (jnp.sum(gap * gap), 0, eye - half_upper(gap)))
-    settled = (size <= 1e-6) & (jnp.min(jnp.where(r == c, y, 1.0)) > 0.0)
+        _, e, y, count = state
+        return (*measured(y - close(y, half_upper(e))), count + 1)
+
+    size, _, y, _ = lax.while_loop(more, newton, (*measured(eye - half_upper(gap)), 0))
+    settled = (size <= 1e-7) & (jnp.min(jnp.where(r == c, y, 1.0)) > 0.0)
 
     @pl.when(settled)
     def _():
@@ -492,7 +517,7 @@
             pltpu.VMEM((RING * SLOTS + 1, B, B), F32),
             pltpu.VMEM((VRING, 2 * B, K), F32),
         ]
-        + [pltpu.SemaphoreType.DMA((RING,)), pltpu.SemaphoreType.DMA((VRING,))],
+        + [pltpu.SemaphoreType.DMA((RING, 2)), pltpu.SemaphoreType.DMA((VRING,))],
         compiler_params=params(16),
         cost_estimate=cost(flops * 2, 24 * 2**20),
         name="first_inner",
@@ -509,12 +534,12 @@
         name="first_edge",
     )(columns, *sent, *got, part, uh, ul, hh, hl, vh, vl)
 
-    def inner(vectors, prior):
+    def inner(vectors, prior, *gram):
         return pl.pallas_call(
             inner_kernel,
-            out_shape=(slab, slab, partial),
+            out_shape=(slab, slab, partial) + gram,
             in_specs=(VM,) * 6,
-            out_specs=(VM,) * 3,
+            out_specs=(VM,) * (3 + len(gram)),
             compiler_params=params(6),
             cost_estimate=cost(flops, 2**20),
             name="inner",
@@ -534,18 +559,18 @@
     )(columns, xh, xl, *got, part, wh, wl, hh, hl, uh, ul)
 
     got = swap_pairs(far, near)
-    fh, fl, part = inner((wh, wl), (uh, ul))
+    fh, fl, part, inside = inner((wh, wl), (uh, ul), pltpu.VMEM((2, K, K), F32))
     half = pltpu.VMEM((B + 8, B), F32)
     fh, fl, mine, theirs = pl.pallas_call(
         last_edge_kernel,
         out_shape=(slab, slab, half, half),
-        in_specs=(SM,) + (VM,) * 7,
+        in_specs=(SM,) + (VM,) * 8,
         out_specs=(VM,) * 4,
         input_output_aliases={6: 0, 7: 1},
         compiler_params=params(8),
         cost_estimate=cost(2e9, 2 * 2**20),
         name="last_edge_gram",
-    )(columns, xh, xl, *got, part, fh, fl)
+    )(columns, xh, xl, *got, part, fh, fl, inside)
 
     swap = [(0, 1), (1, 0)]
     mine = mine + lax.ppermute(theirs, "c", swap)

time: 210 us -> 210 us (level)
  no operation moved by 1% of the time
where the time goes in v3:
time: 210 us; the launch traced here: 209 us
  Pallas kernels  158 us (75%)
  starting transfers between devices  38.3 us (18%)
  waiting for transfers between devices  11.9 us (6%)
    pallas_call x1, Pallas kernels, body(): pl.pallas_call(basis_kernel, out_shape=(jax.ShapeDtypeStruct((LOCAL, K),...  118 us
    ppermute x9, starting transfers between devices, group_sum(): lax.ppermute(value, axis, [(i, i ^ k) for i in range(count)])  20.5 us
    pallas_call x2, Pallas kernels, inner(): pl.pallas_call(inner_kernel, out_shape=(slab, slab, partial) + gram, in_s...  16.2 us
    pallas_call x1, Pallas kernels, body(): pl.pallas_call(first_kernel, out_shape=(wide, wide, slab, slab, slab, sla...  14.7 us
    ppermute x3, starting transfers between devices, swap_pairs(): got_far = lax.ppermute(far, ALL, pairs + [(j, i) for i, j in pairs])  12.6 us
    ppermute x9, waiting for transfers between devices, group_sum(): lax.ppermute(value, axis, [(i, i ^ k) for i in range(count)])  10.1 us
    ppermute x1, starting transfers between devices, body(): other = lax.ppermute(mine, 'c', swap)  4.22 us
  transfers between devices with their start and end apart: 17, of which 8 were waited for; matrix products, arithmetic and copies ran while one was open for 0% of the time, Pallas kernels for 15%

profile of v3, /device:TPU:1, one launch (start us, length us, event | category | flops | bytes accessed | tf_op | source)
XLA Modules:
  0.0 209.4 jit_solution(6753886912251122976)
XLA Ops:
  0.6 3.2 %pack_edges.1 = (f32[2304,128]{1,0:T(8,128)S(1)}, f32[2304,128]{1,0:T(8,128)S(1)}) custom-call(s32[8,32]{1,0:T(8,128)} %bitcast.4, s32[32]{0:T(128)} %counts.3, f32[256,128,128]{2,1,0:T(8,128)} %bitcast.2, f32[4096,256]{1,0:T(8,128)} %vectors.3), custom_call_target="tpu_custom_call" | custom-call | bytes 4718592 | tf_op jit(solution)/shard_map/pack_edges/pallas_call | solution.py:488
  3.9 4.6 %collective-permute-start = (f32[2304,128]{1,0:T(8,128)S(1)}, f32[2304,128]{1,0:T(8,128)S(1)}, u32[]{:S(2)}, u32[]{:S(2)}) collective-permute-start(f32[2304,128]{1,0:T(8,128)S(1)} %get-tuple-element.32.sent_far), channel_id=1, source_target_pairs={{1,2},{3,4},{5,6},{7,8},{9,10},{11,12},{13,14},{15,16},{17,18},{19... | collective-permute-start | bytes 3538952 | tf_op jit(solution)/shard_map/ppermute | solution.py:469
  8.6 14.7 %first_inner.1 = (bf16[16,256,1280]{2,1,0:T(8,128)(2,1)S(1)}, bf16[16,256,1280]{2,1,0:T(8,128)(2,1)S(1)}, bf16[4096,256]{1,0:T(8,128)(2,1)S(1)}, bf16[4096,256]{...) custom-call(s32[8,32]{1,0:T(8,128)} %bitcast.5, ...), custom_call_target="tpu_custom_call" | custom-call | flops 16106127360 | bytes 25165824 | tf_op jit(solution)/shard_map/first_inner/pallas_call | solution.py:510
  23.3 2.2 %first_edge.1 = (bf16[4096,256]{1,0:T(8,128)(2,1)S(1)}, bf16[4096,256]{1,0:T(8,128)(2,1)S(1)}, bf16[2,512,512]{2,1,0:T(8,128)(2,1)S(1)}, bf16[2,512,512]{2,1,0:T...) custom-call(s32[8,32]{1,0:T(8,128)} %bitcast.6, ...), custom_call_target="tpu_custom_call", output_to_operand_aliasing={{0}: (6, {}), {1}: (7, {})} | custom-call | flops 800000000 | bytes 6291456 | tf_op jit(solution)/shard_map/first_edge/pallas_call | solution.py:526
  25.6 4.9 %collective-permute-start.2 = (f32[512,256]{1,0:T(8,128)S(1)}, f32[512,256]{1,0:T(8,128)S(1)}, u32[]{:S(2)}, u32[]{:S(2)}) collective-permute-start(f32[512,256]{1,0:T(8,128)S(1)} %get-tuple-element.43), channel_id=1, source_target_pairs={{1,2},{3,4},{5,6},{7,8},{9,10},{11,12},{13,14},{15,16},{17,18},{19... | collective-permute-start | bytes 1572872 | tf_op jit(solution)/shard_map/ppermute | solution.py:469
  30.7 7.7 %inner.2 = (bf16[4096,256]{1,0:T(8,128)(2,1)S(1)}, bf16[4096,256]{1,0:T(8,128)(2,1)S(1)}, f32[1024,256]{1,0:T(8,128)S(1)}) custom-call(bf16[16,256,1280]{2,1,0:T(8,128)(2,1)S(1)} %get-tuple-element.37.rest_0_.hh, bf16[16,256,1280]{2,1,0:T(8,128)(2,1)S(1)} %get-tuple-element.38.rest_1_.hl, bf16[4096,256]{1,0:T(8,128)(2,1)S(1)} %get-tuple-element.45.vh.rest_2_.ph, ...), custom_call_target="tpu_custom_call" | custom-call | flops 8053063680 | bytes 1048576 | tf_op jit(solution)/shard_map/inner/pallas_call | solution.py:538
  38.4 1.8 edge.1
  40.3 3.1 %collective-permute-start.4 = (f32[512,256]{1,0:T(8,128)S(1)}, f32[512,256]{1,0:T(8,128)S(1)}, u32[]{:S(2)}, u32[]{:S(2)}) collective-permute-start(f32[512,256]{1,0:T(8,128)S(1)} %get-tuple-element.50), channel_id=1, source_target_pairs={{1,2},{3,4},{5,6},{7,8},{9,10},{11,12},{13,14},{15,16},{17,18},{19... | collective-permute-start | bytes 1572872 | tf_op jit(solution)/shard_map/ppermute | solution.py:469
  43.5 8.5 %inner.3 = (bf16[4096,256]{1,0:T(8,128)(2,1)S(1)}, bf16[4096,256]{1,0:T(8,128)(2,1)S(1)}, f32[1024,256]{1,0:T(8,128)S(1)}, f32[2,256,256]{2,1,0:T(8,128)S(1)}) custom-call(bf16[16,256,1280]{2,1,0:T(8,128)(2,1)S(1)} %get-tuple-element.37.rest_0_.hh, bf16[16,256,1280]{2,1,0:T(8,128)(2,1)S(1)} %get-tuple-element.38.rest_1_.hl, ...), custom_call_target="tpu_custom_call" | custom-call | flops 8053063680 | bytes 1048576 | tf_op jit(solution)/shard_map/inner/pallas_call | solution.py:538
  52.0 2.2 %last_edge_gram.1 = (bf16[4096,256]{1,0:T(8,128)(2,1)S(1)}, bf16[4096,256]{1,0:T(8,128)(2,1)S(1)}, f32[136,128]{1,0:T(8,128)S(1)}, f32[136,128]{1,0:T(8,128)S(1)}) custom-call(s32[8,32]{1,0:T(8,128)} %bitcast.8, bf16[2,512,512]{2,1,0:T(8,128)(2,1)S(1)} %get-tuple-element.41.xh, ...), custom_call_target="tpu_custom_call", output_to_operand_aliasing={{0}: (6, {}), {1}: (7, {})} | custom-call | flops 2000000000 | bytes 2097152 | tf_op jit(solution)/shard_map/last_edge_gram/pallas_call | solution.py:564
  54.8 0.9 collective-permute-done.6
  55.8 12.4 %collective-permute-start.9 = (f32[136,128]{1,0:T(8,128)S(1)}, f32[136,128]{1,0:T(8,128)S(1)}, u32[]{:S(2)}, u32[]{:S(2)}) collective-permute-start(f32[136,128]{1,0:T(8,128)S(1)} %add.30), channel_id=1, source_target_pairs={{0,96},{32,64},{64,32},{96,0},{1,97},{33,65},{65,33},{97,1},{2,98}... | collective-permute-start | bytes 208904 | tf_op jit(solution)/shard_map/ppermute | solution.py:477
  68.1 1.0 collective-permute-start.8
  69.2 1.9 collective-permute-done.9
  71.0 1.7 collective-permute-done.8
  73.0 3.1 %collective-permute-start.10 = (f32[136,128]{1,0:T(8,128)S(1)}, f32[136,128]{1,0:T(8,128)S(1)}, u32[]{:S(2)}, u32[]{:S(2)}) collective-permute-start(f32[136,128]{1,0:T(8,128)S(1)} %add_add_fusion.2), channel_id=1, source_target_pairs={{0,8},{8,0},{16,24},{24,16},{1,9},{9,1},{17,25},{25,17},{2,10},{10... | collective-permute-start | bytes 208904 | tf_op jit(solution)/shard_map/ppermute | solution.py:477
  76.2 1.9 collective-permute-done.12
  78.6 3.1 %collective-permute-start.15 = (f32[136,128]{1,0:T(8,128)S(1)}, f32[136,128]{1,0:T(8,128)S(1)}, u32[]{:S(2)}, u32[]{:S(2)}) collective-permute-start(f32[136,128]{1,0:T(8,128)S(1)} %add_add_fusion.1), channel_id=1, source_target_pairs={{0,6},{2,4},{4,2},{6,0},{1,7},{3,5},{5,3},{7,1},{8,14},{10,12},{12... | collective-permute-start | bytes 208904 | tf_op jit(solution)/shard_map/ppermute | solution.py:477
  81.7 0.7 collective-permute-start.13
  82.4 1.3 collective-permute-done.15
  83.7 2.7 %collective-permute-done.14 = f32[136,128]{1,0:T(8,128)S(1)} collective-permute-done((f32[136,128]{1,0:T(8,128)S(1)}, f32[136,128]{1,0:T(8,128)S(1)}, u32[]{:S(2)}, u32[]{:S(2)}) %collective-permute-start.14) | collective-permute-done | bytes 69664 | tf_op jit(solution)/shard_map/ppermute | solution.py:477
  86.4 4.2 %collective-permute-start.16 = (f32[136,128]{1,0:T(8,128)S(1)}, f32[136,128]{1,0:T(8,128)S(1)}, u32[]{:S(2)}, u32[]{:S(2)}) collective-permute-start(f32[136,128]{1,0:T(8,128)S(1)} %add_add_fusion.mine), channel_id=1, source_target_pairs={{0,1},{1,0},{2,3},{3,2},{4,5},{5,4},{6,7},{7,6},{8,9},{9,8},{10,11... | collective-permute-start | bytes 208904 | tf_op jit(solution)/shard_map/ppermute | solution.py:579
  90.6 0.9 collective-permute-done.16.other
  91.5 117.7 %basis.1 = (f32[4096,256]{1,0:T(8,128)}, f32[256,256]{1,0:T(8,128)}) custom-call(s32[8,32]{1,0:T(8,128)} %bitcast.9, f32[136,128]{1,0:T(8,128)S(1)} %add_add_fusion.mine, f32[136,128]{1,0:T(8,128)S(1)} %collective-permute-done.16.other, bf16[4096,256]{1,0:T(8,128)(2,1)S(1)} %get-tuple-element.60.uh, bf16[4096,256]{1,0:T(8,128)(2,1)S(1)} %get-tuple-element.61.ul, ...), custom_call_target="tpu_custom_call" | custom-call | flops 2000000000 | bytes 4194304 | tf_op jit(solution)/shard_map/basis/pallas_call | solution.py:583
  (22 shorter events, 1.8 us)
Async XLA Ops:
  3.9 19.4 %collective-permute-start = (f32[2304,128]{1,0:T(8,128)S(1)}, f32[2304,128]{1,0:T(8,128)S(1)}, u32[]{:S(2)}, u32[]{:S(2)}) collective-permute-start(f32[2304,128]{1,0:T(8,128)S(1)} %get-tuple-element.32.sent_far), channel_id=1, source_target_pairs={{1,2},{3,4},{5,6},{7,8},{9,10},{11,12},{13,14},{15,16},{17,18},{19... | collective-permute-start | bytes 3538952 | tf_op jit(solution)/shard_map/ppermute | solution.py:469
  8.5 14.8 %collective-permute-start.1 = (f32[2304,128]{1,0:T(8,128)S(1)}, f32[2304,128]{1,0:T(8,128)S(1)}, u32[]{:S(2)}, u32[]{:S(2)}) collective-permute-start(f32[2304,128]{1,0:T(8,128)S(1)} %get-tuple-element.33.sent_near), channel_id=1, source_target_pairs={{0,1},{1,0},{2,3},{3,2},{4,5},{5,4},{6,7},{7,6},{8,9},{9,8},{10,11... | collective-permute-start | bytes 3538952 | tf_op jit(solution)/shard_map/ppermute | solution.py:470
  25.6 12.9 %collective-permute-start.2 = (f32[512,256]{1,0:T(8,128)S(1)}, f32[512,256]{1,0:T(8,128)S(1)}, u32[]{:S(2)}, u32[]{:S(2)}) collective-permute-start(f32[512,256]{1,0:T(8,128)S(1)} %get-tuple-element.43), channel_id=1, source_target_pairs={{1,2},{3,4},{5,6},{7,8},{9,10},{11,12},{13,14},{15,16},{17,18},{19... | collective-permute-start | bytes 1572872 | tf_op jit(solution)/shard_map/ppermute | solution.py:469
  30.4 8.0 %collective-permute-start.3 = (f32[512,256]{1,0:T(8,128)S(1)}, f32[512,256]{1,0:T(8,128)S(1)}, u32[]{:S(2)}, u32[]{:S(2)}) collective-permute-start(f32[512,256]{1,0:T(8,128)S(1)} %get-tuple-element.44), channel_id=1, source_target_pairs={{0,1},{1,0},{2,3},{3,2},{4,5},{5,4},{6,7},{7,6},{8,9},{9,8},{10,11... | collective-permute-start | bytes 1572872 | tf_op jit(solution)/shard_map/ppermute | solution.py:470
  40.3 11.7 %collective-permute-start.4 = (f32[512,256]{1,0:T(8,128)S(1)}, f32[512,256]{1,0:T(8,128)S(1)}, u32[]{:S(2)}, u32[]{:S(2)}) collective-permute-start(f32[512,256]{1,0:T(8,128)S(1)} %get-tuple-element.50), channel_id=1, source_target_pairs={{1,2},{3,4},{5,6},{7,8},{9,10},{11,12},{13,14},{15,16},{17,18},{19... | collective-permute-start | bytes 1572872 | tf_op jit(solution)/shard_map/ppermute | solution.py:469
  43.4 8.6 %collective-permute-start.5 = (f32[512,256]{1,0:T(8,128)S(1)}, f32[512,256]{1,0:T(8,128)S(1)}, u32[]{:S(2)}, u32[]{:S(2)}) collective-permute-start(f32[512,256]{1,0:T(8,128)S(1)} %get-tuple-element.51), channel_id=1, source_target_pairs={{0,1},{1,0},{2,3},{3,2},{4,5},{5,4},{6,7},{7,6},{8,9},{9,8},{10,11... | collective-permute-start | bytes 1572872 | tf_op jit(solution)/shard_map/ppermute | solution.py:470
  54.3 1.5 collective-permute-start.6
  55.8 15.3 %collective-permute-start.9 = (f32[136,128]{1,0:T(8,128)S(1)}, f32[136,128]{1,0:T(8,128)S(1)}, u32[]{:S(2)}, u32[]{:S(2)}) collective-permute-start(f32[136,128]{1,0:T(8,128)S(1)} %add.30), channel_id=1, source_target_pairs={{0,96},{32,64},{64,32},{96,0},{1,97},{33,65},{65,33},{97,1},{2,98}... | collective-permute-start | bytes 208904 | tf_op jit(solution)/shard_map/ppermute | solution.py:477
  68.1 4.7 %collective-permute-start.8 = (f32[136,128]{1,0:T(8,128)S(1)}, f32[136,128]{1,0:T(8,128)S(1)}, u32[]{:S(2)}, u32[]{:S(2)}) collective-permute-start(f32[136,128]{1,0:T(8,128)S(1)} %add.30), channel_id=1, source_target_pairs={{0,64},{32,96},{64,0},{96,32},{1,65},{33,97},{65,1},{97,33},{2,66}... | collective-permute-start | bytes 208904 | tf_op jit(solution)/shard_map/ppermute | solution.py:477
  69.2 3.6 %collective-permute-start.7 = (f32[136,128]{1,0:T(8,128)S(1)}, f32[136,128]{1,0:T(8,128)S(1)}, u32[]{:S(2)}, u32[]{:S(2)}) collective-permute-start(f32[136,128]{1,0:T(8,128)S(1)} %add.30), channel_id=1, source_target_pairs={{0,32},{32,0},{64,96},{96,64},{1,33},{33,1},{65,97},{97,65},{2,34}... | collective-permute-start | bytes 208904 | tf_op jit(solution)/shard_map/ppermute | solution.py:477
  72.8 5.2 %collective-permute-start.12 = (f32[136,128]{1,0:T(8,128)S(1)}, f32[136,128]{1,0:T(8,128)S(1)}, u32[]{:S(2)}, u32[]{:S(2)}) collective-permute-start(f32[136,128]{1,0:T(8,128)S(1)} %add_add_fusion.2), channel_id=1, source_target_pairs={{0,24},{8,16},{16,8},{24,0},{1,25},{9,17},{17,9},{25,1},{2,26},{10... | collective-permute-start | bytes 208904 | tf_op jit(solution)/shard_map/ppermute | solution.py:477
  72.9 5.1 %collective-permute-start.11 = (f32[136,128]{1,0:T(8,128)S(1)}, f32[136,128]{1,0:T(8,128)S(1)}, u32[]{:S(2)}, u32[]{:S(2)}) collective-permute-start(f32[136,128]{1,0:T(8,128)S(1)} %add_add_fusion.2), channel_id=1, source_target_pairs={{0,16},{8,24},{16,0},{24,8},{1,17},{9,25},{17,1},{25,9},{2,18},{10... | collective-permute-start | bytes 208904 | tf_op jit(solution)/shard_map/ppermute | solution.py:477
  73.0 5.6 %collective-permute-start.10 = (f32[136,128]{1,0:T(8,128)S(1)}, f32[136,128]{1,0:T(8,128)S(1)}, u32[]{:S(2)}, u32[]{:S(2)}) collective-permute-start(f32[136,128]{1,0:T(8,128)S(1)} %add_add_fusion.2), channel_id=1, source_target_pairs={{0,8},{8,0},{16,24},{24,16},{1,9},{9,1},{17,25},{25,17},{2,10},{10... | collective-permute-start | bytes 208904 | tf_op jit(solution)/shard_map/ppermute | solution.py:477
  78.6 5.1 %collective-permute-start.15 = (f32[136,128]{1,0:T(8,128)S(1)}, f32[136,128]{1,0:T(8,128)S(1)}, u32[]{:S(2)}, u32[]{:S(2)}) collective-permute-start(f32[136,128]{1,0:T(8,128)S(1)} %add_add_fusion.1), channel_id=1, source_target_pairs={{0,6},{2,4},{4,2},{6,0},{1,7},{3,5},{5,3},{7,1},{8,14},{10,12},{12... | collective-permute-start | bytes 208904 | tf_op jit(solution)/shard_map/ppermute | solution.py:477
  81.7 4.7 %collective-permute-start.14 = (f32[136,128]{1,0:T(8,128)S(1)}, f32[136,128]{1,0:T(8,128)S(1)}, u32[]{:S(2)}, u32[]{:S(2)}) collective-permute-start(f32[136,128]{1,0:T(8,128)S(1)} %add_add_fusion.1), channel_id=1, source_target_pairs={{0,4},{2,6},{4,0},{6,2},{1,5},{3,7},{5,1},{7,3},{8,12},{10,14},{12... | collective-permute-start | bytes 208904 | tf_op jit(solution)/shard_map/ppermute | solution.py:477
  81.7 4.7 %collective-permute-start.13 = (f32[136,128]{1,0:T(8,128)S(1)}, f32[136,128]{1,0:T(8,128)S(1)}, u32[]{:S(2)}, u32[]{:S(2)}) collective-permute-start(f32[136,128]{1,0:T(8,128)S(1)} %add_add_fusion.1), channel_id=1, source_target_pairs={{0,2},{2,0},{4,6},{6,4},{1,3},{3,1},{5,7},{7,5},{8,10},{10,8},{12,... | collective-permute-start | bytes 208904 | tf_op jit(solution)/shard_map/ppermute | solution.py:477
  86.4 5.1 %collective-permute-start.16 = (f32[136,128]{1,0:T(8,128)S(1)}, f32[136,128]{1,0:T(8,128)S(1)}, u32[]{:S(2)}, u32[]{:S(2)}) collective-permute-start(f32[136,128]{1,0:T(8,128)S(1)} %add_add_fusion.mine), channel_id=1, source_target_pairs={{0,1},{1,0},{2,3},{3,2},{4,5},{5,4},{6,7},{7,6},{8,9},{9,8},{10,11... | collective-permute-start | bytes 208904 | tf_op jit(solution)/shard_map/ppermute | solution.py:579

commit v4 on v3

--- a/solution.py
+++ b/solution.py
@@ -1,3 +1,6 @@
+import functools
+import math
+
 import jax
 import jax.numpy as jnp
 from jax import lax
@@ -69,8 +72,8 @@
         table[k] = DEAD
 
 
-def even_core(columns):
-    return (columns[0, 0] // ROWS) % 2 == 0
+def even_core():
+    return lax.axis_index("c") == 0
 
 
 def pack_kernel(columns, counts, blocks, vectors, swap_far, swap_near, table, zero, sems):
@@ -109,7 +112,7 @@
         for move in moves:
             move.wait()
 
-    even = even_core(columns)
+    even = even_core()
 
     @pl.when(even)
     def _():
@@ -262,20 +265,31 @@
 
 
 def first_edge_kernel(
-    columns, sent_far, sent_near, got_far, got_near, part, uh_in, ul_in, *rest
+    sent_far, sent_near, got_far, got_near, part, uh_in, ul_in, *rest
 ):
     uh, ul, xh, xl, far, near = rest[KEPT:]
     del uh_in, ul_in
-    even = even_core(columns)
-
-    def own(side, at):
-        a, b = sent_far[at, :], sent_near[at, :]
-        return jnp.where(even, a, b) if side == 0 else jnp.where(even, b, a)
-
-    def got(side, at):
-        a, b = got_far[at, :], got_near[at, :]
-        return jnp.where(even, a, b) if side == 0 else jnp.where(even, b, a)
-
+    by_side(
+        functools.partial(first_edges, part, uh, ul, xh, xl),
+        (sent_far, sent_near),
+        (got_far, got_near),
+        (far, near),
+    )
+
+
+def by_side(work, *pairs):
+    even = even_core()
+
+    @pl.when(even)
+    def _():
+        work(*pairs)
+
+    @pl.when(jnp.logical_not(even))
+    def _():
+        work(*((near, far) for far, near in pairs))
+
+
+def first_edges(part, uh, ul, xh, xl, own, got, out):
     zero = jnp.zeros((B, B), BF16)
     for r in range(REACH):
         for c in range(REACH):
@@ -288,50 +302,41 @@
                     else:
                         a = PAIRS_NEXT.index((28 + r, 4 + c - r)) * B
                         b = PAIRS_PREV.index((c, r - c - 4)) * B
-                    parts = split(own(side, slice(a, a + B)) + got(side, slice(b, b + B)).T)
+                    parts = split(own[side][a : a + B, :] + got[side][b : b + B, :].T)
                 else:
                     parts = (zero, zero)
                 xh[side, at, cols], xl[side, at, cols] = parts
-    values = []
     for side in range(2):
         halves = [
-            split(got(side, slice(10 * B + half * EDGE, 10 * B + (half + 1) * EDGE)))
-            for half in range(2)
+            split(got[side][10 * B + half * EDGE : 10 * B + (half + 1) * EDGE, :]) for half in range(2)
         ]
         high = jnp.concatenate([halves[0][0], halves[1][0]], axis=1)
         low = jnp.concatenate([halves[0][1], halves[1][1]], axis=1)
         value = part[side * EDGE : (side + 1) * EDGE, :] + 0.5 * cross(xh, xl, side, high, low)
         write_edge(side, value, uh, ul)
-        values.append(value)
-    send_edges(even, values, far, near)
-
-
-def send_edges(even, values, far, near):
-    far[...] = jnp.where(even, values[0], values[1])
-    near[...] = jnp.where(even, values[1], values[0])
-
-
-def finish_edges(columns, xh, xl, got_far, got_near, part, uh, ul):
-    even = even_core(columns)
-    a, b = got_far[...], got_near[...]
-    values = []
-    for side, halo in enumerate((jnp.where(even, a, b), jnp.where(even, b, a))):
-        value = part[side * EDGE : (side + 1) * EDGE, :] + cross(xh, xl, side, *split(halo))
+        out[side][...] = value
+
+
+def finish_edges(xh, xl, part, uh, ul, got, out=()):
+    for side in range(2):
+        halo = split(got[side][...])
+        value = part[side * EDGE : (side + 1) * EDGE, :] + cross(xh, xl, side, *halo)
         write_edge(side, value, uh, ul)
-        values.append(value)
-    return even, values
-
-
-def edge_kernel(columns, xh, xl, got_far, got_near, part, uh_in, ul_in, *rest):
+        if out:
+            out[side][...] = value
+
+
+def edge_kernel(xh, xl, got_far, got_near, part, uh_in, ul_in, *rest):
     uh, ul, far, near = rest[KEPT:]
     del uh_in, ul_in
-    even, values = finish_edges(columns, xh, xl, got_far, got_near, part, uh, ul)
-    send_edges(even, values, far, near)
-
-
-def last_edge_kernel(columns, xh, xl, got_far, got_near, part, uh_in, ul_in, inside, uh, ul, mine, theirs):
+    work = functools.partial(finish_edges, xh, xl, part, uh, ul)
+    by_side(work, (got_far, got_near), (far, near))
+
+
+def last_edge_kernel(xh, xl, got_far, got_near, part, uh_in, ul_in, inside, uh, ul, mine, theirs):
     del uh_in, ul_in
-    even, _ = finish_edges(columns, xh, xl, got_far, got_near, part, uh, ul)
+    even = even_core()
+    by_side(functools.partial(finish_edges, xh, xl, part, uh, ul), (got_far, got_near))
     first = gram_parts(slice(0, EDGE), uh, ul)
     last = gram_parts(slice(LOCAL - EDGE, LOCAL), uh, ul)
     main, mixed = (inside[k] + (first[k] + last[k]) for k in range(2))
@@ -363,10 +368,10 @@
     return product(ah, bh) + (product(ah, bl) + product(al, bh))
 
 
-def basis_kernel(columns, mine, other, uh, ul, scale, basis, factor, work, upper, inverse, out, sems):
+def basis_kernel(root, mine, other, uh, ul, basis, factor, work, upper, inverse, out, sems):
     r = lax.broadcasted_iota(jnp.int32, (B, B), 0)
     c = lax.broadcasted_iota(jnp.int32, (B, B), 1)
-    even = even_core(columns)
+    even = even_core()
     ad = jnp.where(even, mine[...], other[...])
     b = jnp.where(even, other[:B, :], mine[:B, :])
     square = ad[:B, :]
@@ -444,7 +449,6 @@
 
         lax.fori_loop(0, K, back, 0)
 
-    root = scale[0]
     factor[...] = upper[...] * (row_d * row_s) / root
     wh, wl = split(inverse[...] * (col_s * root))
 
@@ -526,13 +530,13 @@
     uh, ul, xh, xl, far, near = pl.pallas_call(
         first_edge_kernel,
         out_shape=(slab, slab, crossing, crossing, edge, edge),
-        in_specs=(SM,) + (VM,) * (7 + KEPT),
+        in_specs=(VM,) * (7 + KEPT),
         out_specs=(VM,) * 6,
-        input_output_aliases={6: 0, 7: 1},
+        input_output_aliases={5: 0, 6: 1},
         compiler_params=params(4),
         cost_estimate=cost(8e8, 6 * 2**20),
         name="first_edge",
-    )(columns, *sent, *got, part, uh, ul, hh, hl, vh, vl)
+    )(*sent, *got, part, uh, ul, hh, hl, vh, vl)
 
     def inner(vectors, prior, *gram):
         return pl.pallas_call(
@@ -550,13 +554,13 @@
     wh, wl, far, near = pl.pallas_call(
         edge_kernel,
         out_shape=(slab, slab, edge, edge),
-        in_specs=(SM,) + (VM,) * (7 + KEPT),
+        in_specs=(VM,) * (7 + KEPT),
         out_specs=(VM,) * 4,
-        input_output_aliases={6: 0, 7: 1},
+        input_output_aliases={5: 0, 6: 1},
         compiler_params=params(8),
         cost_estimate=cost(8e8, 2 * 2**20),
         name="edge",
-    )(columns, xh, xl, *got, part, wh, wl, hh, hl, uh, ul)
+    )(xh, xl, *got, part, wh, wl, hh, hl, uh, ul)
 
     got = swap_pairs(far, near)
     fh, fl, part, inside = inner((wh, wl), (uh, ul), pltpu.VMEM((2, K, K), F32))
@@ -564,13 +568,13 @@
     fh, fl, mine, theirs = pl.pallas_call(
         last_edge_kernel,
         out_shape=(slab, slab, half, half),
-        in_specs=(SM,) + (VM,) * 8,
+        in_specs=(VM,) * 8,
         out_specs=(VM,) * 4,
-        input_output_aliases={6: 0, 7: 1},
+        input_output_aliases={5: 0, 6: 1},
         compiler_params=params(8),
         cost_estimate=cost(2e9, 2 * 2**20),
         name="last_edge_gram",
-    )(columns, xh, xl, *got, part, fh, fl, inside)
+    )(xh, xl, *got, part, fh, fl, inside)
 
     swap = [(0, 1), (1, 0)]
     mine = mine + lax.ppermute(theirs, "c", swap)
@@ -579,18 +583,17 @@
     other = lax.ppermute(mine, "c", swap)
 
     total_rows = LOCAL * lax.axis_size(ALL)
-    scale = jnp.sqrt(jnp.float32(total_rows)).reshape(1)
     basis, factor = pl.pallas_call(
-        basis_kernel,
+        functools.partial(basis_kernel, math.sqrt(total_rows)),
         out_shape=(jax.ShapeDtypeStruct((LOCAL, K), F32), jax.ShapeDtypeStruct((K, K), F32)),
-        in_specs=(SM, VM, VM, VM, VM, SM),
+        in_specs=(VM,) * 4,
         out_specs=(HB, VM),
         scratch_shapes=[pltpu.VMEM((K, K), F32)] * 3
         + [pltpu.VMEM((LOCAL, K), F32), pltpu.SemaphoreType.DMA((LOCAL // CHUNK,))],
         compiler_params=params(12),
         cost_estimate=cost(2e9, 4 * 2**20),
         name="basis",
-    )(columns, mine, other, fh, fl, scale)
+    )(mine, other, fh, fl)
     return basis, factor
 
 

time: 210 us -> 206 us (0.981)
  Pallas kernels: 158 us -> 154 us
where the time goes in v4:
time: 206 us
  Pallas kernels  154 us (75%)
  starting transfers between devices  38.7 us (19%)
  waiting for transfers between devices  11.9 us (6%)
    pallas_call x1, Pallas kernels, body(): pl.pallas_call(functools.partial(basis_kernel, math.sqrt(total_rows)), ou...  117 us
    ppermute x9, starting transfers between devices, group_sum(): lax.ppermute(value, axis, [(i, i ^ k) for i in range(count)])  20.6 us
    pallas_call x2, Pallas kernels, inner(): pl.pallas_call(inner_kernel, out_shape=(slab, slab, partial) + gram, in_s...  16.2 us
    pallas_call x1, Pallas kernels, body(): pl.pallas_call(first_kernel, out_shape=(wide, wide, slab, slab, slab, sla...  14.2 us
    ppermute x3, starting transfers between devices, swap_pairs(): got_far = lax.ppermute(far, ALL, pairs + [(j, i) for i, j in pairs])  13.1 us
    ppermute x9, waiting for transfers between devices, group_sum(): lax.ppermute(value, axis, [(i, i ^ k) for i in range(count)])  10.1 us
  transfers between devices with their start and end apart: 17, of which 8 were waited for; matrix products, arithmetic and copies ran while one was open for 0% of the time, Pallas kernels for 15%

profile of v4, /device:TPU:1, one launch (start us, length us, event | category | flops | bytes accessed | tf_op | source)
XLA Modules:
  0.0 206.1 jit_solution(7781554875190933581)
XLA Ops:
  0.6 3.0 %pack_edges.1 = (f32[2304,128]{1,0:T(8,128)S(1)}, f32[2304,128]{1,0:T(8,128)S(1)}) custom-call(s32[8,32]{1,0:T(8,128)} %bitcast.4, s32[32]{0:T(128)} %counts.3, f32[256,128,128]{2,1,0:T(8,128)} %bitcast.2, f32[4096,256]{1,0:T(8,128)} %vectors.3), custom_call_target="tpu_custom_call" | custom-call | bytes 4718592 | tf_op jit(solution)/shard_map/pack_edges/pallas_call | solution.py:492
  3.7 4.6 %collective-permute-start = (f32[2304,128]{1,0:T(8,128)S(1)}, f32[2304,128]{1,0:T(8,128)S(1)}, u32[]{:S(2)}, u32[]{:S(2)}) collective-permute-start(f32[2304,128]{1,0:T(8,128)S(1)} %get-tuple-element.32.sent_far), channel_id=1, source_target_pairs={{1,2},{3,4},{5,6},{7,8},{9,10},{11,12},{13,14},{15,16},{17,18},{19... | collective-permute-start | bytes 3538952 | tf_op jit(solution)/shard_map/ppermute | solution.py:473
  8.4 14.2 %first_inner.1 = (bf16[16,256,1280]{2,1,0:T(8,128)(2,1)S(1)}, bf16[16,256,1280]{2,1,0:T(8,128)(2,1)S(1)}, bf16[4096,256]{1,0:T(8,128)(2,1)S(1)}, bf16[4096,256]{...) custom-call(s32[8,32]{1,0:T(8,128)} %bitcast.5, ...), custom_call_target="tpu_custom_call" | custom-call | flops 16106127360 | bytes 25165824 | tf_op jit(solution)/shard_map/first_inner/pallas_call | solution.py:514
  22.6 1.5 first_edge.1
  24.2 4.9 %collective-permute-start.2 = (f32[512,256]{1,0:T(8,128)S(1)}, f32[512,256]{1,0:T(8,128)S(1)}, u32[]{:S(2)}, u32[]{:S(2)}) collective-permute-start(f32[512,256]{1,0:T(8,128)S(1)} %get-tuple-element.43), channel_id=1, source_target_pairs={{1,2},{3,4},{5,6},{7,8},{9,10},{11,12},{13,14},{15,16},{17,18},{19... | collective-permute-start | bytes 1572872 | tf_op jit(solution)/shard_map/ppermute | solution.py:473
  29.1 7.7 %inner.2 = (bf16[4096,256]{1,0:T(8,128)(2,1)S(1)}, bf16[4096,256]{1,0:T(8,128)(2,1)S(1)}, f32[1024,256]{1,0:T(8,128)S(1)}) custom-call(bf16[16,256,1280]{2,1,0:T(8,128)(2,1)S(1)} %get-tuple-element.37.rest_0_.hh, bf16[16,256,1280]{2,1,0:T(8,128)(2,1)S(1)} %get-tuple-element.38.rest_1_.hl, bf16[4096,256]{1,0:T(8,128)(2,1)S(1)} %get-tuple-element.45.vh.rest_2_.ph, ...), custom_call_target="tpu_custom_call" | custom-call | flops 8053063680 | bytes 1048576 | tf_op jit(solution)/shard_map/inner/pallas_call | solution.py:542
  36.9 1.0 edge.1
  37.9 3.6 %collective-permute-start.4 = (f32[512,256]{1,0:T(8,128)S(1)}, f32[512,256]{1,0:T(8,128)S(1)}, u32[]{:S(2)}, u32[]{:S(2)}) collective-permute-start(f32[512,256]{1,0:T(8,128)S(1)} %get-tuple-element.50), channel_id=1, source_target_pairs={{1,2},{3,4},{5,6},{7,8},{9,10},{11,12},{13,14},{15,16},{17,18},{19... | collective-permute-start | bytes 1572872 | tf_op jit(solution)/shard_map/ppermute | solution.py:473
  41.8 8.5 %inner.3 = (bf16[4096,256]{1,0:T(8,128)(2,1)S(1)}, bf16[4096,256]{1,0:T(8,128)(2,1)S(1)}, f32[1024,256]{1,0:T(8,128)S(1)}, f32[2,256,256]{2,1,0:T(8,128)S(1)}) custom-call(bf16[16,256,1280]{2,1,0:T(8,128)(2,1)S(1)} %get-tuple-element.37.rest_0_.hh, bf16[16,256,1280]{2,1,0:T(8,128)(2,1)S(1)} %get-tuple-element.38.rest_1_.hl, ...), custom_call_target="tpu_custom_call" | custom-call | flops 8053063680 | bytes 1048576 | tf_op jit(solution)/shard_map/inner/pallas_call | solution.py:542
  50.3 1.6 last_edge_gram.1
  52.5 0.9 collective-permute-done.6
  53.4 13.3 %collective-permute-start.9 = (f32[136,128]{1,0:T(8,128)S(1)}, f32[136,128]{1,0:T(8,128)S(1)}, u32[]{:S(2)}, u32[]{:S(2)}) collective-permute-start(f32[136,128]{1,0:T(8,128)S(1)} %add.30), channel_id=1, source_target_pairs={{0,96},{32,64},{64,32},{96,0},{1,97},{33,65},{65,33},{97,1},{2,98}... | collective-permute-start | bytes 208904 | tf_op jit(solution)/shard_map/ppermute | solution.py:481
  66.7 0.7 collective-permute-start.7
  67.4 2.0 collective-permute-done.9
  69.4 2.0 collective-permute-done.8
  71.6 3.1 %collective-permute-start.10 = (f32[136,128]{1,0:T(8,128)S(1)}, f32[136,128]{1,0:T(8,128)S(1)}, u32[]{:S(2)}, u32[]{:S(2)}) collective-permute-start(f32[136,128]{1,0:T(8,128)S(1)} %add_add_fusion.2), channel_id=1, source_target_pairs={{0,8},{8,0},{16,24},{24,16},{1,9},{9,1},{17,25},{25,17},{2,10},{10... | collective-permute-start | bytes 208904 | tf_op jit(solution)/shard_map/ppermute | solution.py:481
  74.7 1.9 collective-permute-done.12
  77.2 2.3 %collective-permute-start.15 = (f32[136,128]{1,0:T(8,128)S(1)}, f32[136,128]{1,0:T(8,128)S(1)}, u32[]{:S(2)}, u32[]{:S(2)}) collective-permute-start(f32[136,128]{1,0:T(8,128)S(1)} %add_add_fusion.1), channel_id=1, source_target_pairs={{0,6},{2,4},{4,2},{6,0},{1,7},{3,5},{5,3},{7,1},{8,14},{10,12},{12... | collective-permute-start | bytes 208904 | tf_op jit(solution)/shard_map/ppermute | solution.py:481
  79.5 1.0 collective-permute-start.13
  80.5 1.1 collective-permute-done.15
  81.6 2.5 %collective-permute-done.14 = f32[136,128]{1,0:T(8,128)S(1)} collective-permute-done((f32[136,128]{1,0:T(8,128)S(1)}, f32[136,128]{1,0:T(8,128)S(1)}, u32[]{:S(2)}, u32[]{:S(2)}) %collective-permute-start.14) | collective-permute-done | bytes 69664 | tf_op jit(solution)/shard_map/ppermute | solution.py:481
  84.2 3.9 %collective-permute-start.16 = (f32[136,128]{1,0:T(8,128)S(1)}, f32[136,128]{1,0:T(8,128)S(1)}, u32[]{:S(2)}, u32[]{:S(2)}) collective-permute-start(f32[136,128]{1,0:T(8,128)S(1)} %add_add_fusion.mine), channel_id=1, source_target_pairs={{0,1},{1,0},{2,3},{3,2},{4,5},{5,4},{6,7},{7,6},{8,9},{9,8},{10,11... | collective-permute-start | bytes 208904 | tf_op jit(solution)/shard_map/ppermute | solution.py:583
  88.1 0.9 collective-permute-done.16.other
  89.0 116.9 %basis.1 = (f32[4096,256]{1,0:T(8,128)}, f32[256,256]{1,0:T(8,128)}) custom-call(f32[136,128]{1,0:T(8,128)S(1)} %add_add_fusion.mine, f32[136,128]{1,0:T(8,128)S(1)} %collective-permute-done.16.other, bf16[4096,256]{1,0:T(8,128)(2,1)S(1)} %get-tuple-element.60.uh, bf16[4096,256]{1,0:T(8,128)(2,1)S(1)} %get-tuple-element.61.ul), custom_call_target="tpu_custom_call" | custom-call | flops 2000000000 | bytes 4194304 | tf_op jit(solution)/shard_map/basis/pallas_call | solution.py:586
  (22 shorter events, 1.9 us)
Async XLA Ops:
  3.7 19.0 %collective-permute-start = (f32[2304,128]{1,0:T(8,128)S(1)}, f32[2304,128]{1,0:T(8,128)S(1)}, u32[]{:S(2)}, u32[]{:S(2)}) collective-permute-start(f32[2304,128]{1,0:T(8,128)S(1)} %get-tuple-element.32.sent_far), channel_id=1, source_target_pairs={{1,2},{3,4},{5,6},{7,8},{9,10},{11,12},{13,14},{15,16},{17,18},{19... | collective-permute-start | bytes 3538952 | tf_op jit(solution)/shard_map/ppermute | solution.py:473
  8.3 14.3 %collective-permute-start.1 = (f32[2304,128]{1,0:T(8,128)S(1)}, f32[2304,128]{1,0:T(8,128)S(1)}, u32[]{:S(2)}, u32[]{:S(2)}) collective-permute-start(f32[2304,128]{1,0:T(8,128)S(1)} %get-tuple-element.33.sent_near), channel_id=1, source_target_pairs={{0,1},{1,0},{2,3},{3,2},{4,5},{5,4},{6,7},{7,6},{8,9},{9,8},{10,11... | collective-permute-start | bytes 3538952 | tf_op jit(solution)/shard_map/ppermute | solution.py:474
  24.2 12.7 %collective-permute-start.2 = (f32[512,256]{1,0:T(8,128)S(1)}, f32[512,256]{1,0:T(8,128)S(1)}, u32[]{:S(2)}, u32[]{:S(2)}) collective-permute-start(f32[512,256]{1,0:T(8,128)S(1)} %get-tuple-element.43), channel_id=1, source_target_pairs={{1,2},{3,4},{5,6},{7,8},{9,10},{11,12},{13,14},{15,16},{17,18},{19... | collective-permute-start | bytes 1572872 | tf_op jit(solution)/shard_map/ppermute | solution.py:473
  29.0 7.8 %collective-permute-start.3 = (f32[512,256]{1,0:T(8,128)S(1)}, f32[512,256]{1,0:T(8,128)S(1)}, u32[]{:S(2)}, u32[]{:S(2)}) collective-permute-start(f32[512,256]{1,0:T(8,128)S(1)} %get-tuple-element.44), channel_id=1, source_target_pairs={{0,1},{1,0},{2,3},{3,2},{4,5},{5,4},{6,7},{7,6},{8,9},{9,8},{10,11... | collective-permute-start | bytes 1572872 | tf_op jit(solution)/shard_map/ppermute | solution.py:474
  37.9 12.4 %collective-permute-start.4 = (f32[512,256]{1,0:T(8,128)S(1)}, f32[512,256]{1,0:T(8,128)S(1)}, u32[]{:S(2)}, u32[]{:S(2)}) collective-permute-start(f32[512,256]{1,0:T(8,128)S(1)} %get-tuple-element.50), channel_id=1, source_target_pairs={{1,2},{3,4},{5,6},{7,8},{9,10},{11,12},{13,14},{15,16},{17,18},{19... | collective-permute-start | bytes 1572872 | tf_op jit(solution)/shard_map/ppermute | solution.py:473
  41.5 8.8 %collective-permute-start.5 = (f32[512,256]{1,0:T(8,128)S(1)}, f32[512,256]{1,0:T(8,128)S(1)}, u32[]{:S(2)}, u32[]{:S(2)}) collective-permute-start(f32[512,256]{1,0:T(8,128)S(1)} %get-tuple-element.51), channel_id=1, source_target_pairs={{0,1},{1,0},{2,3},{3,2},{4,5},{5,4},{6,7},{7,6},{8,9},{9,8},{10,11... | collective-permute-start | bytes 1572872 | tf_op jit(solution)/shard_map/ppermute | solution.py:474
  51.9 1.5 collective-permute-start.6
  53.4 16.0 %collective-permute-start.9 = (f32[136,128]{1,0:T(8,128)S(1)}, f32[136,128]{1,0:T(8,128)S(1)}, u32[]{:S(2)}, u32[]{:S(2)}) collective-permute-start(f32[136,128]{1,0:T(8,128)S(1)} %add.30), channel_id=1, source_target_pairs={{0,96},{32,64},{64,32},{96,0},{1,97},{33,65},{65,33},{97,1},{2,98}... | collective-permute-start | bytes 208904 | tf_op jit(solution)/shard_map/ppermute | solution.py:481
  66.7 4.7 %collective-permute-start.8 = (f32[136,128]{1,0:T(8,128)S(1)}, f32[136,128]{1,0:T(8,128)S(1)}, u32[]{:S(2)}, u32[]{:S(2)}) collective-permute-start(f32[136,128]{1,0:T(8,128)S(1)} %add.30), channel_id=1, source_target_pairs={{0,64},{32,96},{64,0},{96,32},{1,65},{33,97},{65,1},{97,33},{2,66}... | collective-permute-start | bytes 208904 | tf_op jit(solution)/shard_map/ppermute | solution.py:481
  66.7 4.7 %collective-permute-start.7 = (f32[136,128]{1,0:T(8,128)S(1)}, f32[136,128]{1,0:T(8,128)S(1)}, u32[]{:S(2)}, u32[]{:S(2)}) collective-permute-start(f32[136,128]{1,0:T(8,128)S(1)} %add.30), channel_id=1, source_target_pairs={{0,32},{32,0},{64,96},{96,64},{1,33},{33,1},{65,97},{97,65},{2,34}... | collective-permute-start | bytes 208904 | tf_op jit(solution)/shard_map/ppermute | solution.py:481
  71.4 5.2 %collective-permute-start.12 = (f32[136,128]{1,0:T(8,128)S(1)}, f32[136,128]{1,0:T(8,128)S(1)}, u32[]{:S(2)}, u32[]{:S(2)}) collective-permute-start(f32[136,128]{1,0:T(8,128)S(1)} %add_add_fusion.2), channel_id=1, source_target_pairs={{0,24},{8,16},{16,8},{24,0},{1,25},{9,17},{17,9},{25,1},{2,26},{10... | collective-permute-start | bytes 208904 | tf_op jit(solution)/shard_map/ppermute | solution.py:481
  71.5 5.1 %collective-permute-start.11 = (f32[136,128]{1,0:T(8,128)S(1)}, f32[136,128]{1,0:T(8,128)S(1)}, u32[]{:S(2)}, u32[]{:S(2)}) collective-permute-start(f32[136,128]{1,0:T(8,128)S(1)} %add_add_fusion.2), channel_id=1, source_target_pairs={{0,16},{8,24},{16,0},{24,8},{1,17},{9,25},{17,1},{25,9},{2,18},{10... | collective-permute-start | bytes 208904 | tf_op jit(solution)/shard_map/ppermute | solution.py:481
  71.6 5.6 %collective-permute-start.10 = (f32[136,128]{1,0:T(8,128)S(1)}, f32[136,128]{1,0:T(8,128)S(1)}, u32[]{:S(2)}, u32[]{:S(2)}) collective-permute-start(f32[136,128]{1,0:T(8,128)S(1)} %add_add_fusion.2), channel_id=1, source_target_pairs={{0,8},{8,0},{16,24},{24,16},{1,9},{9,1},{17,25},{25,17},{2,10},{10... | collective-permute-start | bytes 208904 | tf_op jit(solution)/shard_map/ppermute | solution.py:481
  77.2 4.5 %collective-permute-start.15 = (f32[136,128]{1,0:T(8,128)S(1)}, f32[136,128]{1,0:T(8,128)S(1)}, u32[]{:S(2)}, u32[]{:S(2)}) collective-permute-start(f32[136,128]{1,0:T(8,128)S(1)} %add_add_fusion.1), channel_id=1, source_target_pairs={{0,6},{2,4},{4,2},{6,0},{1,7},{3,5},{5,3},{7,1},{8,14},{10,12},{12... | collective-permute-start | bytes 208904 | tf_op jit(solution)/shard_map/ppermute | solution.py:481
  79.5 4.7 %collective-permute-start.14 = (f32[136,128]{1,0:T(8,128)S(1)}, f32[136,128]{1,0:T(8,128)S(1)}, u32[]{:S(2)}, u32[]{:S(2)}) collective-permute-start(f32[136,128]{1,0:T(8,128)S(1)} %add_add_fusion.1), channel_id=1, source_target_pairs={{0,4},{2,6},{4,0},{6,2},{1,5},{3,7},{5,1},{7,3},{8,12},{10,14},{12... | collective-permute-start | bytes 208904 | tf_op jit(solution)/shard_map/ppermute | solution.py:481
  79.5 4.7 %collective-permute-start.13 = (f32[136,128]{1,0:T(8,128)S(1)}, f32[136,128]{1,0:T(8,128)S(1)}, u32[]{:S(2)}, u32[]{:S(2)}) collective-permute-start(f32[136,128]{1,0:T(8,128)S(1)} %add_add_fusion.1), channel_id=1, source_target_pairs={{0,2},{2,0},{4,6},{6,4},{1,3},{3,1},{5,7},{7,5},{8,10},{10,8},{12,... | collective-permute-start | bytes 208904 | tf_op jit(solution)/shard_map/ppermute | solution.py:481
  84.2 4.8 %collective-permute-start.16 = (f32[136,128]{1,0:T(8,128)S(1)}, f32[136,128]{1,0:T(8,128)S(1)}, u32[]{:S(2)}, u32[]{:S(2)}) collective-permute-start(f32[136,128]{1,0:T(8,128)S(1)} %add_add_fusion.mine), channel_id=1, source_target_pairs={{0,1},{1,0},{2,3},{3,2},{4,5},{5,4},{6,7},{7,6},{8,9},{9,8},{10,11... | collective-permute-start | bytes 208904 | tf_op jit(solution)/shard_map/ppermute | solution.py:583

commit v5 on v4

--- a/solution.py
+++ b/solution.py
@@ -76,25 +76,48 @@
     return lax.axis_index("c") == 0
 
 
-def pack_kernel(columns, counts, blocks, vectors, swap_far, swap_near, table, zero, sems):
-    first = columns[0, 0]
+def scalar_copies(columns_in, counts_in, columns, counts, sems):
+    return (
+        pltpu.make_async_copy(columns_in, columns, sems.at[0]),
+        pltpu.make_async_copy(counts_in, counts, sems.at[1]),
+    )
+
+
+def pack_kernel(
+    columns_in, counts_in, blocks, vectors, swap_far, swap_near, columns, counts, table, zero, sems, scalar_sems
+):
+    scalars = scalar_copies(columns_in, counts_in, columns, counts, scalar_sems)
+    for copy in scalars:
+        copy.start()
+
+    def vector_moves(to_prev, to_next):
+        return [
+            pltpu.make_async_copy(
+                vectors.at[pl.ds(start, EDGE), pl.ds(half * B, B)],
+                out.at[pl.ds(10 * B + half * EDGE, EDGE), :],
+                sems.at[side * 12 + 10 + half],
+            )
+            for side, (out, start) in enumerate(((to_prev, 0), (to_next, LOCAL - EDGE)))
+            for half in range(2)
+        ]
+
+    def begin(pair):
+        for move in vector_moves(*pair):
+            move.start()
+
+    by_side(begin, (swap_far, swap_near))
     zero[...] = jnp.zeros_like(zero)
     for r in (0, 1, 2, 3, 28, 29, 30, 31):
         clear_table(table, place(r, -4), place(r, 5))
+    for copy in scalars:
+        copy.wait()
+    first = columns[0, 0]
+    for r in (0, 1, 2, 3, 28, 29, 30, 31):
         fill_table(table, columns, counts, first, r)
 
-    def fill(to_prev, to_next):
-        moves = []
-        for side, (out, pairs) in enumerate(((to_prev, PAIRS_PREV), (to_next, PAIRS_NEXT))):
-            start = 0 if side == 0 else LOCAL - EDGE
-            for half in range(2):
-                move = pltpu.make_async_copy(
-                    vectors.at[pl.ds(start, EDGE), pl.ds(half * B, B)],
-                    out.at[pl.ds(10 * B + half * EDGE, EDGE), :],
-                    sems.at[side * 12 + 10 + half],
-                )
-                move.start()
-                moves.append(move)
+    def fill(pair):
+        moves = vector_moves(*pair)
+        for side, (out, pairs) in enumerate(zip(pair, (PAIRS_PREV, PAIRS_NEXT))):
             for k, (r, o) in enumerate(pairs):
                 slot = table[place(r, o)]
                 target = out.at[pl.ds(k * B, B), :]
@@ -112,15 +135,7 @@
         for move in moves:
             move.wait()
 
-    even = even_core()
-
-    @pl.when(even)
-    def _():
-        fill(swap_far, swap_near)
-
-    @pl.when(jnp.logical_not(even))
-    def _():
-        fill(swap_near, swap_far)
+    by_side(fill, (swap_far, swap_near))
 
 
 def window_of(p):
@@ -144,27 +159,31 @@
 
 
 def first_kernel(
-    columns, counts, blocks, vectors, hh, hl, vh, vl, uh, ul, part, table, sbuf, vbuf, ssem, vsem
+    columns_in, counts_in, blocks, vectors, hh, hl, vh, vl, uh, ul, part,
+    columns, counts, table, sbuf, vbuf, ssem, vsem, scalar_sems,
 ):
     class block_copy:
         def __init__(self, r):
-            self.more = counts[r] > SLOTS // 2
-            self.parts = [
-                pltpu.make_async_copy(
-                    blocks.at[pl.ds(r * SLOTS + k * 4, SLOTS // 2)],
-                    sbuf.at[pl.ds((r % RING) * SLOTS + k * 4, SLOTS // 2)],
-                    ssem.at[r % RING, k],
-                )
-                for k in range(2)
-            ]
+            self.row = r
+
+        def part(self, k):
+            r = self.row
+            return pltpu.make_async_copy(
+                blocks.at[pl.ds(r * SLOTS + k * 4, SLOTS // 2)],
+                sbuf.at[pl.ds((r % RING) * SLOTS + k * 4, SLOTS // 2)],
+                ssem.at[r % RING, k],
+            )
 
         def start(self):
-            self.parts[0].start()
-            pl.when(self.more)(self.parts[1].start)
+            self.part(0).start()
+            self.start_more()
+
+        def start_more(self):
+            pl.when(counts[self.row] > SLOTS // 2)(lambda: self.part(1).start())
 
         def wait(self):
-            self.parts[0].wait()
-            pl.when(self.more)(self.parts[1].wait)
+            self.part(0).wait()
+            pl.when(counts[self.row] > SLOTS // 2)(lambda: self.part(1).wait())
 
     def vector_copy(q):
         return pltpu.make_async_copy(
@@ -176,11 +195,18 @@
         at = rows(q * 2 * B, 2 * B)
         vh[at, :], vl[at, :] = split(vbuf[q % VRING])
 
+    scalars = scalar_copies(columns_in, counts_in, columns, counts, scalar_sems)
+    for copy in scalars:
+        copy.start()
     for r in range(RING):
-        block_copy(r).start()
+        block_copy(r).part(0).start()
         if r % 2 and r // 2 < VRING:
             vector_copy(r // 2).start()
     sbuf[RING * SLOTS] = jnp.zeros((B, B), F32)
+    for copy in scalars:
+        copy.wait()
+    for r in range(RING):
+        block_copy(r).start_more()
     first = columns[0, 0]
 
     def clear(r, _):
@@ -492,12 +518,15 @@
     sent = pl.pallas_call(
         pack_kernel,
         out_shape=(packed, packed),
-        in_specs=(SM, SM, HB, HB),
+        in_specs=(HB,) * 4,
         out_specs=(VM, VM),
         scratch_shapes=[
+            pltpu.SMEM((SLOTS, ROWS), jnp.int32),
+            pltpu.SMEM((ROWS,), jnp.int32),
             pltpu.SMEM((TABLE + 1,), jnp.int32),
             pltpu.VMEM((B, B), F32),
             pltpu.SemaphoreType.DMA((24,)),
+            pltpu.SemaphoreType.DMA((2,)),
         ],
         compiler_params=params(2),
         cost_estimate=cost(0, 2 * 2 * PACKED * B * 4),
@@ -514,14 +543,17 @@
     hh, hl, vh, vl, uh, ul, part = pl.pallas_call(
         first_kernel,
         out_shape=(wide, wide, slab, slab, slab, slab, partial),
-        in_specs=(SM, SM, HB, HB),
+        in_specs=(HB,) * 4,
         out_specs=(VM,) * 7,
         scratch_shapes=[
+            pltpu.SMEM((SLOTS, ROWS), jnp.int32),
+            pltpu.SMEM((ROWS,), jnp.int32),
             pltpu.SMEM((TABLE + 1,), jnp.int32),
             pltpu.VMEM((RING * SLOTS + 1, B, B), F32),
             pltpu.VMEM((VRING, 2 * B, K), F32),
         ]
-        + [pltpu.SemaphoreType.DMA((RING, 2)), pltpu.SemaphoreType.DMA((VRING,))],
+        + [pltpu.SemaphoreType.DMA((RING, 2)), pltpu.SemaphoreType.DMA((VRING,))]
+        + [pltpu.SemaphoreType.DMA((2,))],
         compiler_params=params(16),
         cost_estimate=cost(flops * 2, 24 * 2**20),
         name="first_inner",

time: 206 us -> 207 us (level)
  no operation moved by 1% of the time
where the time goes in v5:
time: 207 us; the launch traced here: 206 us
  Pallas kernels  155 us (75%)
  starting transfers between devices  38.2 us (18%)
  waiting for transfers between devices  11.8 us (6%)
    pallas_call x1, Pallas kernels, body(): pl.pallas_call(functools.partial(basis_kernel, math.sqrt(total_rows)), ou...  117 us
    ppermute x9, starting transfers between devices, group_sum(): lax.ppermute(value, axis, [(i, i ^ k) for i in range(count)])  20.4 us
    pallas_call x2, Pallas kernels, inner(): pl.pallas_call(inner_kernel, out_shape=(slab, slab, partial) + gram, in_s...  16.2 us
    pallas_call x1, Pallas kernels, body(): pl.pallas_call(first_kernel, out_shape=(wide, wide, slab, slab, slab, sla...  14.6 us
    ppermute x3, starting transfers between devices, swap_pairs(): got_far = lax.ppermute(far, ALL, pairs + [(j, i) for i, j in pairs])  12.5 us
    ppermute x9, waiting for transfers between devices, group_sum(): lax.ppermute(value, axis, [(i, i ^ k) for i in range(count)])  10 us
    ppermute x1, starting transfers between devices, body(): other = lax.ppermute(mine, 'c', swap)  4.29 us
  transfers between devices with their start and end apart: 17, of which 8 were waited for; matrix products, arithmetic and copies ran while one was open for 0% of the time, Pallas kernels for 15%

profile of v5, /device:TPU:1, one launch (start us, length us, event | category | flops | bytes accessed | tf_op | source)
XLA Modules:
  0.0 206.1 jit_solution(5299064433202923308)
XLA Ops:
  0.6 3.2 %pack_edges.1 = (f32[2304,128]{1,0:T(8,128)S(1)}, f32[2304,128]{1,0:T(8,128)S(1)}) custom-call(s32[8,32]{1,0:T(8,128)} %bitcast.4, s32[32]{0:T(128)} %counts_in.3, f32[256,128,128]{2,1,0:T(8,128)} %bitcast.2, f32[4096,256]{1,0:T(8,128)} %vectors.3), custom_call_target="tpu_custom_call" | custom-call | bytes 4718592 | tf_op jit(solution)/shard_map/pack_edges/pallas_call | solution.py:518
  3.8 4.4 %collective-permute-start = (f32[2304,128]{1,0:T(8,128)S(1)}, f32[2304,128]{1,0:T(8,128)S(1)}, u32[]{:S(2)}, u32[]{:S(2)}) collective-permute-start(f32[2304,128]{1,0:T(8,128)S(1)} %get-tuple-element.32.sent_far), channel_id=1, source_target_pairs={{1,2},{3,4},{5,6},{7,8},{9,10},{11,12},{13,14},{15,16},{17,18},{19... | collective-permute-start | bytes 3538952 | tf_op jit(solution)/shard_map/ppermute | solution.py:499
  8.3 14.6 %first_inner.1 = (bf16[16,256,1280]{2,1,0:T(8,128)(2,1)S(1)}, bf16[16,256,1280]{2,1,0:T(8,128)(2,1)S(1)}, bf16[4096,256]{1,0:T(8,128)(2,1)S(1)}, bf16[4096,256]{...) custom-call(s32[8,32]{1,0:T(8,128)} %bitcast.5, ...), custom_call_target="tpu_custom_call" | custom-call | flops 16106127360 | bytes 25165824 | tf_op jit(solution)/shard_map/first_inner/pallas_call | solution.py:543
  22.9 1.5 first_edge.1
  24.4 4.5 %collective-permute-start.2 = (f32[512,256]{1,0:T(8,128)S(1)}, f32[512,256]{1,0:T(8,128)S(1)}, u32[]{:S(2)}, u32[]{:S(2)}) collective-permute-start(f32[512,256]{1,0:T(8,128)S(1)} %get-tuple-element.43), channel_id=1, source_target_pairs={{1,2},{3,4},{5,6},{7,8},{9,10},{11,12},{13,14},{15,16},{17,18},{19... | collective-permute-start | bytes 1572872 | tf_op jit(solution)/shard_map/ppermute | solution.py:499
  29.1 7.7 %inner.2 = (bf16[4096,256]{1,0:T(8,128)(2,1)S(1)}, bf16[4096,256]{1,0:T(8,128)(2,1)S(1)}, f32[1024,256]{1,0:T(8,128)S(1)}) custom-call(bf16[16,256,1280]{2,1,0:T(8,128)(2,1)S(1)} %get-tuple-element.37.rest_0_.hh, bf16[16,256,1280]{2,1,0:T(8,128)(2,1)S(1)} %get-tuple-element.38.rest_1_.hl, bf16[4096,256]{1,0:T(8,128)(2,1)S(1)} %get-tuple-element.45.vh.rest_2_.ph, ...), custom_call_target="tpu_custom_call" | custom-call | flops 8053063680 | bytes 1048576 | tf_op jit(solution)/shard_map/inner/pallas_call | solution.py:574
  36.8 1.0 edge.1
  37.8 3.6 %collective-permute-start.4 = (f32[512,256]{1,0:T(8,128)S(1)}, f32[512,256]{1,0:T(8,128)S(1)}, u32[]{:S(2)}, u32[]{:S(2)}) collective-permute-start(f32[512,256]{1,0:T(8,128)S(1)} %get-tuple-element.50), channel_id=1, source_target_pairs={{1,2},{3,4},{5,6},{7,8},{9,10},{11,12},{13,14},{15,16},{17,18},{19... | collective-permute-start | bytes 1572872 | tf_op jit(solution)/shard_map/ppermute | solution.py:499
  41.7 8.5 %inner.3 = (bf16[4096,256]{1,0:T(8,128)(2,1)S(1)}, bf16[4096,256]{1,0:T(8,128)(2,1)S(1)}, f32[1024,256]{1,0:T(8,128)S(1)}, f32[2,256,256]{2,1,0:T(8,128)S(1)}) custom-call(bf16[16,256,1280]{2,1,0:T(8,128)(2,1)S(1)} %get-tuple-element.37.rest_0_.hh, bf16[16,256,1280]{2,1,0:T(8,128)(2,1)S(1)} %get-tuple-element.38.rest_1_.hl, ...), custom_call_target="tpu_custom_call" | custom-call | flops 8053063680 | bytes 1048576 | tf_op jit(solution)/shard_map/inner/pallas_call | solution.py:574
  50.3 1.6 last_edge_gram.1
  52.4 0.9 collective-permute-done.6
  53.3 13.1 %collective-permute-start.9 = (f32[136,128]{1,0:T(8,128)S(1)}, f32[136,128]{1,0:T(8,128)S(1)}, u32[]{:S(2)}, u32[]{:S(2)}) collective-permute-start(f32[136,128]{1,0:T(8,128)S(1)} %add.30), channel_id=1, source_target_pairs={{0,96},{32,64},{64,32},{96,0},{1,97},{33,65},{65,33},{97,1},{2,98}... | collective-permute-start | bytes 208904 | tf_op jit(solution)/shard_map/ppermute | solution.py:507
  67.1 2.0 collective-permute-done.9
  69.0 2.0 collective-permute-done.8
  71.3 3.1 %collective-permute-start.10 = (f32[136,128]{1,0:T(8,128)S(1)}, f32[136,128]{1,0:T(8,128)S(1)}, u32[]{:S(2)}, u32[]{:S(2)}) collective-permute-start(f32[136,128]{1,0:T(8,128)S(1)} %add_add_fusion.2), channel_id=1, source_target_pairs={{0,8},{8,0},{16,24},{24,16},{1,9},{9,1},{17,25},{25,17},{2,10},{10... | collective-permute-start | bytes 208904 | tf_op jit(solution)/shard_map/ppermute | solution.py:507
  74.4 1.9 collective-permute-done.12
  76.3 0.6 collective-permute-done.10
  76.9 2.2 %collective-permute-start.15 = (f32[136,128]{1,0:T(8,128)S(1)}, f32[136,128]{1,0:T(8,128)S(1)}, u32[]{:S(2)}, u32[]{:S(2)}) collective-permute-start(f32[136,128]{1,0:T(8,128)S(1)} %add_add_fusion.1), channel_id=1, source_target_pairs={{0,6},{2,4},{4,2},{6,0},{1,7},{3,5},{5,3},{7,1},{8,14},{10,12},{12... | collective-permute-start | bytes 208904 | tf_op jit(solution)/shard_map/ppermute | solution.py:507
  79.1 1.1 collective-permute-start.13
  80.2 1.1 collective-permute-done.15
  81.3 2.5 %collective-permute-done.14 = f32[136,128]{1,0:T(8,128)S(1)} collective-permute-done((f32[136,128]{1,0:T(8,128)S(1)}, f32[136,128]{1,0:T(8,128)S(1)}, u32[]{:S(2)}, u32[]{:S(2)}) %collective-permute-start.14) | collective-permute-done | bytes 69664 | tf_op jit(solution)/shard_map/ppermute | solution.py:507
  83.8 4.3 %collective-permute-start.16 = (f32[136,128]{1,0:T(8,128)S(1)}, f32[136,128]{1,0:T(8,128)S(1)}, u32[]{:S(2)}, u32[]{:S(2)}) collective-permute-start(f32[136,128]{1,0:T(8,128)S(1)} %add_add_fusion.mine), channel_id=1, source_target_pairs={{0,1},{1,0},{2,3},{3,2},{4,5},{5,4},{6,7},{7,6},{8,9},{9,8},{10,11... | collective-permute-start | bytes 208904 | tf_op jit(solution)/shard_map/ppermute | solution.py:615
  88.1 0.9 collective-permute-done.16.other
  89.0 116.9 %basis.1 = (f32[4096,256]{1,0:T(8,128)}, f32[256,256]{1,0:T(8,128)}) custom-call(f32[136,128]{1,0:T(8,128)S(1)} %add_add_fusion.mine, f32[136,128]{1,0:T(8,128)S(1)} %collective-permute-done.16.other, bf16[4096,256]{1,0:T(8,128)(2,1)S(1)} %get-tuple-element.60.uh, bf16[4096,256]{1,0:T(8,128)(2,1)S(1)} %get-tuple-element.61.ul), custom_call_target="tpu_custom_call" | custom-call | flops 2000000000 | bytes 4194304 | tf_op jit(solution)/shard_map/basis/pallas_call | solution.py:618
  (22 shorter events, 2.0 us)
Async XLA Ops:
  3.8 19.1 %collective-permute-start = (f32[2304,128]{1,0:T(8,128)S(1)}, f32[2304,128]{1,0:T(8,128)S(1)}, u32[]{:S(2)}, u32[]{:S(2)}) collective-permute-start(f32[2304,128]{1,0:T(8,128)S(1)} %get-tuple-element.32.sent_far), channel_id=1, source_target_pairs={{1,2},{3,4},{5,6},{7,8},{9,10},{11,12},{13,14},{15,16},{17,18},{19... | collective-permute-start | bytes 3538952 | tf_op jit(solution)/shard_map/ppermute | solution.py:499
  8.2 14.7 %collective-permute-start.1 = (f32[2304,128]{1,0:T(8,128)S(1)}, f32[2304,128]{1,0:T(8,128)S(1)}, u32[]{:S(2)}, u32[]{:S(2)}) collective-permute-start(f32[2304,128]{1,0:T(8,128)S(1)} %get-tuple-element.33.sent_near), channel_id=1, source_target_pairs={{0,1},{1,0},{2,3},{3,2},{4,5},{5,4},{6,7},{7,6},{8,9},{9,8},{10,11... | collective-permute-start | bytes 3538952 | tf_op jit(solution)/shard_map/ppermute | solution.py:500
  24.4 12.3 %collective-permute-start.2 = (f32[512,256]{1,0:T(8,128)S(1)}, f32[512,256]{1,0:T(8,128)S(1)}, u32[]{:S(2)}, u32[]{:S(2)}) collective-permute-start(f32[512,256]{1,0:T(8,128)S(1)} %get-tuple-element.43), channel_id=1, source_target_pairs={{1,2},{3,4},{5,6},{7,8},{9,10},{11,12},{13,14},{15,16},{17,18},{19... | collective-permute-start | bytes 1572872 | tf_op jit(solution)/shard_map/ppermute | solution.py:499
  29.0 7.8 %collective-permute-start.3 = (f32[512,256]{1,0:T(8,128)S(1)}, f32[512,256]{1,0:T(8,128)S(1)}, u32[]{:S(2)}, u32[]{:S(2)}) collective-permute-start(f32[512,256]{1,0:T(8,128)S(1)} %get-tuple-element.44), channel_id=1, source_target_pairs={{0,1},{1,0},{2,3},{3,2},{4,5},{5,4},{6,7},{7,6},{8,9},{9,8},{10,11... | collective-permute-start | bytes 1572872 | tf_op jit(solution)/shard_map/ppermute | solution.py:500
  37.8 12.4 %collective-permute-start.4 = (f32[512,256]{1,0:T(8,128)S(1)}, f32[512,256]{1,0:T(8,128)S(1)}, u32[]{:S(2)}, u32[]{:S(2)}) collective-permute-start(f32[512,256]{1,0:T(8,128)S(1)} %get-tuple-element.50), channel_id=1, source_target_pairs={{1,2},{3,4},{5,6},{7,8},{9,10},{11,12},{13,14},{15,16},{17,18},{19... | collective-permute-start | bytes 1572872 | tf_op jit(solution)/shard_map/ppermute | solution.py:499
  41.4 8.8 %collective-permute-start.5 = (f32[512,256]{1,0:T(8,128)S(1)}, f32[512,256]{1,0:T(8,128)S(1)}, u32[]{:S(2)}, u32[]{:S(2)}) collective-permute-start(f32[512,256]{1,0:T(8,128)S(1)} %get-tuple-element.51), channel_id=1, source_target_pairs={{0,1},{1,0},{2,3},{3,2},{4,5},{5,4},{6,7},{7,6},{8,9},{9,8},{10,11... | collective-permute-start | bytes 1572872 | tf_op jit(solution)/shard_map/ppermute | solution.py:500
  51.8 1.5 collective-permute-start.6
  53.3 15.7 %collective-permute-start.9 = (f32[136,128]{1,0:T(8,128)S(1)}, f32[136,128]{1,0:T(8,128)S(1)}, u32[]{:S(2)}, u32[]{:S(2)}) collective-permute-start(f32[136,128]{1,0:T(8,128)S(1)} %add.30), channel_id=1, source_target_pairs={{0,96},{32,64},{64,32},{96,0},{1,97},{33,65},{65,33},{97,1},{2,98}... | collective-permute-start | bytes 208904 | tf_op jit(solution)/shard_map/ppermute | solution.py:507
  66.4 4.7 %collective-permute-start.8 = (f32[136,128]{1,0:T(8,128)S(1)}, f32[136,128]{1,0:T(8,128)S(1)}, u32[]{:S(2)}, u32[]{:S(2)}) collective-permute-start(f32[136,128]{1,0:T(8,128)S(1)} %add.30), channel_id=1, source_target_pairs={{0,64},{32,96},{64,0},{96,32},{1,65},{33,97},{65,1},{97,33},{2,66}... | collective-permute-start | bytes 208904 | tf_op jit(solution)/shard_map/ppermute | solution.py:507
  66.5 4.5 %collective-permute-start.7 = (f32[136,128]{1,0:T(8,128)S(1)}, f32[136,128]{1,0:T(8,128)S(1)}, u32[]{:S(2)}, u32[]{:S(2)}) collective-permute-start(f32[136,128]{1,0:T(8,128)S(1)} %add.30), channel_id=1, source_target_pairs={{0,32},{32,0},{64,96},{96,64},{1,33},{33,1},{65,97},{97,65},{2,34}... | collective-permute-start | bytes 208904 | tf_op jit(solution)/shard_map/ppermute | solution.py:507
  71.1 5.2 %collective-permute-start.12 = (f32[136,128]{1,0:T(8,128)S(1)}, f32[136,128]{1,0:T(8,128)S(1)}, u32[]{:S(2)}, u32[]{:S(2)}) collective-permute-start(f32[136,128]{1,0:T(8,128)S(1)} %add_add_fusion.2), channel_id=1, source_target_pairs={{0,24},{8,16},{16,8},{24,0},{1,25},{9,17},{17,9},{25,1},{2,26},{10... | collective-permute-start | bytes 208904 | tf_op jit(solution)/shard_map/ppermute | solution.py:507
  71.2 5.1 %collective-permute-start.11 = (f32[136,128]{1,0:T(8,128)S(1)}, f32[136,128]{1,0:T(8,128)S(1)}, u32[]{:S(2)}, u32[]{:S(2)}) collective-permute-start(f32[136,128]{1,0:T(8,128)S(1)} %add_add_fusion.2), channel_id=1, source_target_pairs={{0,16},{8,24},{16,0},{24,8},{1,17},{9,25},{17,1},{25,9},{2,18},{10... | collective-permute-start | bytes 208904 | tf_op jit(solution)/shard_map/ppermute | solution.py:507
  71.3 5.6 %collective-permute-start.10 = (f32[136,128]{1,0:T(8,128)S(1)}, f32[136,128]{1,0:T(8,128)S(1)}, u32[]{:S(2)}, u32[]{:S(2)}) collective-permute-start(f32[136,128]{1,0:T(8,128)S(1)} %add_add_fusion.2), channel_id=1, source_target_pairs={{0,8},{8,0},{16,24},{24,16},{1,9},{9,1},{17,25},{25,17},{2,10},{10... | collective-permute-start | bytes 208904 | tf_op jit(solution)/shard_map/ppermute | solution.py:507
  76.9 4.5 %collective-permute-start.15 = (f32[136,128]{1,0:T(8,128)S(1)}, f32[136,128]{1,0:T(8,128)S(1)}, u32[]{:S(2)}, u32[]{:S(2)}) collective-permute-start(f32[136,128]{1,0:T(8,128)S(1)} %add_add_fusion.1), channel_id=1, source_target_pairs={{0,6},{2,4},{4,2},{6,0},{1,7},{3,5},{5,3},{7,1},{8,14},{10,12},{12... | collective-permute-start | bytes 208904 | tf_op jit(solution)/shard_map/ppermute | solution.py:507
  79.1 4.7 %collective-permute-start.14 = (f32[136,128]{1,0:T(8,128)S(1)}, f32[136,128]{1,0:T(8,128)S(1)}, u32[]{:S(2)}, u32[]{:S(2)}) collective-permute-start(f32[136,128]{1,0:T(8,128)S(1)} %add_add_fusion.1), channel_id=1, source_target_pairs={{0,4},{2,6},{4,0},{6,2},{1,5},{3,7},{5,1},{7,3},{8,12},{10,14},{12... | collective-permute-start | bytes 208904 | tf_op jit(solution)/shard_map/ppermute | solution.py:507
  79.1 4.7 %collective-permute-start.13 = (f32[136,128]{1,0:T(8,128)S(1)}, f32[136,128]{1,0:T(8,128)S(1)}, u32[]{:S(2)}, u32[]{:S(2)}) collective-permute-start(f32[136,128]{1,0:T(8,128)S(1)} %add_add_fusion.1), channel_id=1, source_target_pairs={{0,2},{2,0},{4,6},{6,4},{1,3},{3,1},{5,7},{7,5},{8,10},{10,8},{12,... | collective-permute-start | bytes 208904 | tf_op jit(solution)/shard_map/ppermute | solution.py:507
  83.8 5.2 %collective-permute-start.16 = (f32[136,128]{1,0:T(8,128)S(1)}, f32[136,128]{1,0:T(8,128)S(1)}, u32[]{:S(2)}, u32[]{:S(2)}) collective-permute-start(f32[136,128]{1,0:T(8,128)S(1)} %add_add_fusion.mine), channel_id=1, source_target_pairs={{0,1},{1,0},{2,3},{3,2},{4,5},{5,4},{6,7},{7,6},{8,9},{9,8},{10,11... | collective-permute-start | bytes 208904 | tf_op jit(solution)/shard_map/ppermute | solution.py:615
